TPU v7x, 128 devices: a whole 4x4x4 slice. The times are simulated.
128 devices in a mesh: lat: 16 (over x, y), lon: 8 (over z, core).
Axes of the slice: x: 4, y: 4, z: 4, core: 2. Of those that a mesh axis runs over, the one named last changes fastest.
Arguments:
- state: bfloat16 [2, 64, 512, 1024], P(None, None, 'lat', 'lon'), may hold values from 3 to 5
- land_mask: int32 [512, 1024], P('lat', 'lon'), may hold values from 0 to 1, as said below
- conv_weight: bfloat16 [3, 3, 64, 64], replicated, may hold values from -0.25 to 0.25
- norm_gain: float32 [64], replicated, may hold values from 0.5 to 1.5
- batchnorm_bias: float32 [64], replicated, may hold values from -0.5 to 0.5
- cotangent: bfloat16 [2, 64, 512, 1024], P(None, None, 'lat', 'lon'), may hold values from -6 to 6
Outputs:
- activated: bfloat16 [2, 64, 512, 1024], P(None, None, 'lat', 'lon')
- state_grad: bfloat16 [2, 64, 512, 1024], P(None, None, 'lat', 'lon')
- weight_grad: float32 [3, 3, 64, 64], replicated
- gain_gradient: float32 [64], replicated
- bias_grad: float32 [64], replicated
Inputs may be any that keep to these rules, and one draw needn't show every extreme that they name: `land_mask`: ocean pixels lie in whole 32 x 32 ocean blocks, with some land pixels among them; land blocks are all 0. The first block of every region of 32 x 128 pixels is an ocean block.
All inputs are finite; a program needn't handle non-finite values.
Results may differ from a plain program's by a relative error of at most 0.00105.
The roundings to bfloat16 on the way count: a program that leaves them out, or rounds other values in their place, can miss the bound.
Values may be sent and summed in bfloat16 or wider, within the bound.
A program may use at most 128 MiB of HBM per device.

v0:
```python
import jax
import jax.numpy as jnp
from jax import lax
from jax.sharding import PartitionSpec as P


def padded_2(cells, sides, width):
    for axis, dim in sides:
        count = lax.axis_size(axis)
        head = lax.slice_in_dim(cells, 0, width, axis=dim)
        tail = lax.slice_in_dim(cells, cells.shape[dim] - width, cells.shape[dim], axis=dim)
        cells = jnp.concatenate(
            [
                lax.ppermute(tail, axis, [(i, (i + 1) % count) for i in range(count)]),
                cells,
                lax.ppermute(head, axis, [((i + 1) % count, i) for i in range(count)]),
            ],
            axis=dim,
        )
    return cells


def clear_poles(padded, width):
    band = lax.axis_index("lat")
    bands = lax.axis_size("lat")
    height = padded.shape[2]
    rows = lax.broadcasted_iota(jnp.int32, (height, 1), 0)
    north = jnp.logical_and(rows < width, band == 0)
    south = jnp.logical_and(rows >= height - width, band == bands - 1)
    keep = jnp.logical_not(jnp.logical_or(north, south)).astype(padded.dtype)
    return padded * keep[None, None]


def valid_conv(padded, kernel):
    return lax.conv_general_dilated(
        padded,
        kernel,
        (1, 1),
        "VALID",
        dimension_numbers=("NCHW", "HWIO", "NCHW"),
        preferred_element_type=jnp.float32,
    )


def kernel_grad(padded, grad):
    raw = lax.conv_general_dilated(
        padded,
        grad,
        (1, 1),
        "VALID",
        dimension_numbers=("CNHW", "IOHW", "NCHW"),
        preferred_element_type=jnp.float32,
    )
    return jnp.transpose(raw, (2, 3, 0, 1))


def on_device(state, land_mask, conv_weight, norm_gain, batchnorm_bias, cotangent):
    maskf = land_mask.astype(jnp.float32)
    full_ocean_mask = maskf[None, None]
    mask_bf = land_mask.astype(jnp.bfloat16)[None, None]
    masked = state * mask_bf
    padded = padded_2(masked, (("lat", 2), ("lon", 3)), 1)
    padded = clear_poles(padded, 1)
    conv = valid_conv(padded, conv_weight)
    cot_use = cotangent.astype(jnp.float32)
    local_count = state.shape[0] * jnp.sum(maskf)
    first, total = lax.psum(
        (jnp.sum(conv * full_ocean_mask, axis=(0, 2, 3)), local_count), ("lat", "lon")
    )
    count = jnp.maximum(total, 1.0)
    mean = first / count
    dev_inner = conv - mean[None, :, None, None]
    spread = lax.psum(
        jnp.sum(dev_inner * dev_inner * full_ocean_mask, axis=(0, 2, 3)), ("lat", "lon")
    )
    var = spread / count
    centered_deviation = conv - mean[None, :, None, None]
    inverse_stddev = lax.rsqrt(var + 1e-05)
    normalized_state = centered_deviation * inverse_stddev[None, :, None, None]
    batchnorm_gain = norm_gain[None, :, None, None]
    preactivation = batchnorm_gain * normalized_state + batchnorm_bias[None, :, None, None]
    sigmoid_pre = jax.nn.sigmoid(preactivation)
    activated = (preactivation * sigmoid_pre * full_ocean_mask).astype(jnp.bfloat16)
    slope = sigmoid_pre * (1.0 + preactivation * (1.0 - sigmoid_pre))
    preactivation_gradient = cot_use * full_ocean_mask * slope
    bias_grad, gain_gradient = lax.psum(
        (
            jnp.sum(preactivation_gradient, axis=(0, 2, 3)),
            jnp.sum(preactivation_gradient * normalized_state, axis=(0, 2, 3)),
        ),
        ("lat", "lon"),
    )
    shifted_first = (norm_gain * bias_grad / count)[None, :, None, None]
    shifted_second = (norm_gain * gain_gradient / count)[None, :, None, None]
    convolution_gradient_map = (
        full_ocean_mask
        * inverse_stddev[None, :, None, None]
        * (
            batchnorm_gain * preactivation_gradient
            - shifted_first
            - normalized_state * shifted_second
        )
    ).astype(jnp.bfloat16)
    grad_padded = padded_2(convolution_gradient_map, (("lat", 2), ("lon", 3)), 1)
    grad_padded = clear_poles(grad_padded, 1)
    flipped = jnp.transpose(conv_weight[::-1, ::-1], (0, 1, 3, 2))
    back = valid_conv(grad_padded, flipped)
    state_grad = (back * full_ocean_mask).astype(jnp.bfloat16)
    local_weight = kernel_grad(padded, convolution_gradient_map)
    weight_grad = lax.psum(local_weight, ("lat", "lon"))
    return (activated, state_grad, weight_grad, gain_gradient, bias_grad)


def solution(mesh):
    return jax.shard_map(
        on_device,
        mesh=mesh,
        in_specs=(
            P(None, None, "lat", "lon"),
            P("lat", "lon"),
            P(),
            P(),
            P(),
            P(None, None, "lat", "lon"),
        ),
        out_specs=(P(None, None, "lat", "lon"), P(None, None, "lat", "lon"), P(), P(), P()),
        check_vma=False,
    )
```

profile of v0, /device:TPU:1, one launch (start us, length us, event | category | flops | bytes accessed | tf_op | source)
XLA Modules:
  0.0 453.3 jit_solution(14636132554922731890)
XLA Ops:
  9.6 2.2 collective-permute-start
  11.8 3.7 collective-permute-start.1
  19.0 3.1 collective-permute-start.2
  22.8 5.4 %copy.105 = bf16[2,64,32,128]{1,2,3,0:T(8,128)(2,1)} copy(bf16[2,64,32,128]{3,2,1,0:T(8,128)(2,1)} %param.11) | data formatting | bytes 2097152 | tf_op args[5]
  28.8 3.7 copy.96
  35.1 2.4 pad.clone
  37.7 3.2 fusion.14
  40.9 3.1 broadcast_select_fusion.1
  47.3 66.6 %all-reduce.1 = (f32[64]{0:T(128)S(1)}, f32[]{:T(128)}) all-reduce(f32[64]{0:T(128)S(1)} %fusion.12, f32[]{:T(128)S(6)} %mul_shard_map.3), channel_id=1, replica_groups=mesh['lat'=16,'lon'=8] {'lat','lon'}, use_global_device_ids=true, to_apply=%region_1.0 | all-reduce | flops 65 | bytes 520 | tf_op jit(solution)/shard_map/psum | solution.py:67
  114.6 2.6 subtract_multiply_fusion.1
  120.0 63.6 %psum.44 = f32[64]{0:T(128)S(1)} all-reduce(f32[64]{0:T(128)S(1)} %fusion.11), channel_id=1, replica_groups=mesh['lat'=16,'lon'=8] {'lat','lon'}, use_global_device_ids=true, to_apply=%region_5.0 | all-reduce | flops 64 | bytes 512 | tf_op jit(solution)/shard_map/psum | solution.py:73
  185.4 3.4 add_multiply_fusion
  194.7 63.0 %all-reduce = (f32[64]{0:T(128)S(1)}, f32[64]{0:T(128)S(1)}) all-reduce(f32[64]{0:T(128)S(1)} %get-tuple-element.26, f32[64]{0:T(128)S(1)} %get-tuple-element.25), channel_id=1, replica_groups=mesh['lat'=16,'lon'=8] {'lat','lon'}, use_global_device_ids=true, to_apply=%region_9.0 | all-reduce | flops 128 | bytes 1024 | tf_op jit(solution)/shard_map/psum | solution.py:86
  257.7 5.5 %broadcast_multiply_fusion = (f32[32,16,17,64]{3,1,2,0:T(8,128)S(1)}, f32[32,16,17,64]{3,1,2,0:T(8,128)}) fusion(f32[32,16,17,64]{3,1,2,0:T(8,128)} %copy-done.2, f32[64]{0:T(128)S(1)} %get-tuple-element.48, f32[64]{0:T(128)S(1)} %copy-done.20, f32[64]{0:T(128)S(1)} %copy-done.17), kind=kLoop, calls=%fused_computation.39 | loop fusion | flops 3899392 | bytes 6685440 | tf_op jit(solution)/shard_map/mul | solution.py:101
  269.2 4.6 %collective-permute-start.5 = (bf16[2,64,1,128]{1,2,3,0:T(2,128)(2,1)S(1)}, bf16[2,64,1,128]{1,2,3,0:T(2,128)(2,1)S(1)}, u32[]{:S(2)}, u32[]{:S(2)}) collective-permute-start(bf16[2,64,1,128]{1,2,3,0:T(2,128)(2,1)S(1)} %get-tuple-element.38), channel_id=1, source_target_pairs={{8,0},{16,8},{24,16},{32,24},{40,32},{48,40},{56,48},{64,56},{72,6... | collective-permute-start | bytes 98312 | tf_op jit(solution)/shard_map/ppermute | solution.py:16
  280.9 15.6 %fusion.22 = f32[3,3,64,64]{3,2,1,0:T(8,128)} fusion(bf16[2,64,34,130]{1,2,3,0:T(8,128)(2,1)S(1)} %maximum_multiply_fusion, bf16[2,64,32,128]{1,2,3,0:T(8,128)(2,1)S(1)} %fusion.6), kind=kOutput, calls=%fused_computation.37 | convolution fusion | flops 603979776 | bytes 2327552 | tf_op jit(solution)/shard_map/transpose | solution.py:54
  296.6 5.9 %copy.103 = f32[32,16,17,64]{3,0,2,1:T(8,128)} copy(f32[32,16,17,64]{3,1,2,0:T(8,128)} %get-tuple-element.34) | data formatting | bytes 4456448 | tf_op jit(solution)/shard_map/mul | solution.py:83
  307.5 2.4 pad.2.clone
  310.1 3.2 fusion.15
  313.3 5.3 %broadcast_select_fusion = f32[32,16,17,64]{3,1,2,0:T(8,128)S(1)} fusion(pred[16,17]{0,1:T(8,128)(4,1)S(1)} %copy-done.24, bf16[3,3,64,64]{3,2,1,0:T(8,128)(2,1)S(1)} %copy-done, bf16[64,34,2,8,19]{0,2,4,3,1:T(2,128)(2,1)S(1)} %fusion.15), kind=kOutput, calls=%fused_computation.40 | convolution fusion | flops 642285568 | bytes 3625232 | tf_op jit(solution)/shard_map/conv_general_dilated | solution.py:35
  320.2 2.2 fusion.25
  322.4 5.2 %copy.119 = bf16[2,64,32,128]{3,2,1,0:T(8,128)(2,1)} copy(bf16[2,64,32,128]{1,2,3,0:T(8,128)(2,1)} %get-tuple-element.44) | data formatting | bytes 2097152
  327.6 3.8 copy.120
  331.4 112.9 %all-reduce.4.cloned.1.call-done = f32[3,3,64,64]{3,2,1,0:T(8,128)} async-done(((f32[3,3,64,64]{3,2,1,0:T(8,128)}), f32[3,3,64,64]{3,2,1,0:T(8,128)}) %all-reduce.4.cloned.1.call-update) | async-done | bytes 147472 | tf_op jit(solution)/shard_map/psum | solution.py:110
  (109 shorter events, 44.2 us)
Async XLA Ops:
  7.2 33.7 %copy-start = (bf16[3,3,64,64]{3,2,1,0:T(8,128)(2,1)S(1)}, bf16[3,3,64,64]{3,2,1,0:T(8,128)(2,1)}, u32[]{:S(2)}) copy-start(bf16[3,3,64,64]{3,2,1,0:T(8,128)(2,1)} %param.8) | copy-start | bytes 221188
  7.2 437.1 %all-reduce.4.cloned.1.call-start = ((), (), s32[]{:S(2)}) async-start(), calls=%async_computation | async-start | bytes 589824 | tf_op jit(solution)/shard_map/psum | solution.py:110
  9.6 7.2 %collective-permute-start = (bf16[2,64,1,128]{3,1,2,0:T(8,128)(2,1)S(1)}, bf16[2,64,1,128]{3,1,2,0:T(8,128)(2,1)S(1)}, u32[]{:S(2)}, u32[]{:S(2)}) collective-permute-start(bf16[2,64,1,128]{3,1,2,0:T(8,128)(2,1)S(1)} %get-tuple-element.41), channel_id=1, source_target_pairs={{0,8},{8,16},{16,24},{24,32},{32,40},{40,48},{48,56},{56,64},{64,7... | collective-permute-start | bytes 98312 | tf_op jit(solution)/shard_map/ppermute | solution.py:14
  11.8 5.0 %collective-permute-start.1 = (bf16[2,64,1,128]{3,1,2,0:T(8,128)(2,1)S(1)}, bf16[2,64,1,128]{3,1,2,0:T(8,128)(2,1)S(1)}, u32[]{:S(2)}, u32[]{:S(2)}) collective-permute-start(bf16[2,64,1,128]{3,1,2,0:T(8,128)(2,1)S(1)} %get-tuple-element.42), channel_id=1, source_target_pairs={{8,0},{16,8},{24,16},{32,24},{40,32},{48,40},{56,48},{64,56},{72,6... | collective-permute-start | bytes 98312 | tf_op jit(solution)/shard_map/ppermute | solution.py:16
  19.0 13.5 %collective-permute-start.2 = (bf16[2,64,34,1]{1,0,3,2:T(2,128)(2,1)S(1)}, bf16[2,64,34,1]{1,0,3,2:T(2,128)(2,1)S(1)}, u32[]{:S(2)}, u32[]{:S(2)}) collective-permute-start(bf16[2,64,34,1]{1,0,3,2:T(2,128)(2,1)S(1)} %copy.121), channel_id=1, source_target_pairs={{0,1},{1,2},{2,3},{3,4},{4,5},{5,6},{6,7},{7,0},{8,9},{9,10},{10,1... | collective-permute-start | bytes 26120 | tf_op jit(solution)/shard_map/ppermute | solution.py:14
  22.6 10.0 %collective-permute-start.3 = (bf16[2,64,34,1]{1,0,3,2:T(2,128)(2,1)S(1)}, bf16[2,64,34,1]{1,0,3,2:T(2,128)(2,1)S(1)}, u32[]{:S(2)}, u32[]{:S(2)}) collective-permute-start(bf16[2,64,34,1]{1,0,3,2:T(2,128)(2,1)S(1)} %copy.122), channel_id=1, source_target_pairs={{1,0},{2,1},{3,2},{4,3},{5,4},{6,5},{7,6},{0,7},{9,8},{10,9},{11,1... | collective-permute-start | bytes 26120 | tf_op jit(solution)/shard_map/ppermute | solution.py:16
  22.6 251.1 %copy-start.18 = (bf16[34]{0:T(256)(128)(2,1)}, bf16[34]{0:T(256)(128)(2,1)S(1)}, u32[]{:S(2)}) copy-start(bf16[34]{0:T(256)(128)(2,1)S(1)} %not_convert_fusion) | copy-start | bytes 208
  22.8 241.9 %copy-start.11 = (f32[32,128]{0,1:T(8,128)}, f32[32,128]{0,1:T(8,128)S(1)}, u32[]{:S(2)}) copy-start(f32[32,128]{0,1:T(8,128)S(1)} %copy.101) | copy-start | bytes 49156
  35.1 5.8 %copy-start.23 = (pred[16,17]{0,1:T(8,128)(4,1)S(1)}, pred[16,17]{0,1:T(8,128)(4,1)}, u32[]{:S(2)}) copy-start(pred[16,17]{0,1:T(8,128)(4,1)} %constant.31) | copy-start | bytes 820
  118.7 66.8 %copy-start.17 = (f32[64]{0:T(128)S(1)}, f32[64]{0:T(128)}, u32[]{:S(2)}) copy-start(f32[64]{0:T(128)} %param.9) | copy-start | bytes 772
  118.7 66.8 %copy-start.20 = (f32[64]{0:T(128)S(1)}, f32[64]{0:T(128)}, u32[]{:S(2)}) copy-start(f32[64]{0:T(128)} %param.10) | copy-start | bytes 772
  257.7 5.5 %copy-start.22 = (f32[64]{0:T(128)}, f32[64]{0:T(128)S(1)}, u32[]{:S(2)}) copy-start(f32[64]{0:T(128)S(1)} %get-tuple-element.53) | copy-start | bytes 772
  268.5 12.4 %copy-start.5 = (bf16[2,64,32,128]{1,2,3,0:T(8,128)(2,1)}, bf16[2,64,32,128]{1,2,3,0:T(8,128)(2,1)S(1)}, u32[]{:S(2)}) copy-start(bf16[2,64,32,128]{1,2,3,0:T(8,128)(2,1)S(1)} %fusion.6) | copy-start | bytes 3145732
  268.8 7.8 %collective-permute-start.4 = (bf16[2,64,1,128]{1,2,3,0:T(2,128)(2,1)S(1)}, bf16[2,64,1,128]{1,2,3,0:T(2,128)(2,1)S(1)}, u32[]{:S(2)}, u32[]{:S(2)}) collective-permute-start(bf16[2,64,1,128]{1,2,3,0:T(2,128)(2,1)S(1)} %get-tuple-element.37), channel_id=1, source_target_pairs={{0,8},{8,16},{16,24},{24,32},{32,40},{40,48},{48,56},{56,64},{64,7... | collective-permute-start | bytes 98312 | tf_op jit(solution)/shard_map/ppermute | solution.py:14
  269.2 7.4 %collective-permute-start.5 = (bf16[2,64,1,128]{1,2,3,0:T(2,128)(2,1)S(1)}, bf16[2,64,1,128]{1,2,3,0:T(2,128)(2,1)S(1)}, u32[]{:S(2)}, u32[]{:S(2)}) collective-permute-start(bf16[2,64,1,128]{1,2,3,0:T(2,128)(2,1)S(1)} %get-tuple-element.38), channel_id=1, source_target_pairs={{8,0},{16,8},{24,16},{32,24},{40,32},{48,40},{56,48},{64,56},{72,6... | collective-permute-start | bytes 98312 | tf_op jit(solution)/shard_map/ppermute | solution.py:16
  278.5 24.1 %collective-permute-start.6 = (bf16[2,64,34,1]{1,0,3,2:T(2,128)(2,1)}, bf16[2,64,34,1]{1,0,3,2:T(2,128)(2,1)}, u32[]{:S(2)}, u32[]{:S(2)}) collective-permute-start(bf16[2,64,34,1]{1,0,3,2:T(2,128)(2,1)} %copy.110), channel_id=1, source_target_pairs={{0,1},{1,2},{2,3},{3,4},{4,5},{5,6},{6,7},{7,0},{8,9},{9,10},{10,1... | collective-permute-start | bytes 26120 | tf_op jit(solution)/shard_map/ppermute | solution.py:14
  280.9 22.3 %collective-permute-start.7 = (bf16[2,64,34,1]{1,0,3,2:T(2,128)(2,1)}, bf16[2,64,34,1]{1,0,3,2:T(2,128)(2,1)}, u32[]{:S(2)}, u32[]{:S(2)}) collective-permute-start(bf16[2,64,34,1]{1,0,3,2:T(2,128)(2,1)} %copy.111), channel_id=1, source_target_pairs={{1,0},{2,1},{3,2},{4,3},{5,4},{6,5},{7,6},{0,7},{9,8},{10,9},{11,1... | collective-permute-start | bytes 26120 | tf_op jit(solution)/shard_map/ppermute | solution.py:16
  296.6 7.4 %copy-start.6 = (bf16[2,64,32,128]{1,2,3,0:T(8,128)(2,1)S(1)}, bf16[2,64,32,128]{1,2,3,0:T(8,128)(2,1)}, u32[]{:S(2)}) copy-start(bf16[2,64,32,128]{1,2,3,0:T(8,128)(2,1)} %copy-done.5) | copy-start | bytes 3145732
  296.6 7.4 %copy-start.14 = (bf16[2,64,1,128]{1,2,3,0:T(2,128)(2,1)S(1)}, bf16[2,64,1,128]{1,2,3,0:T(2,128)(2,1)}, u32[]{:S(2)}) copy-start(bf16[2,64,1,128]{1,2,3,0:T(2,128)(2,1)} %copy-done.13) | copy-start | bytes 98308
  296.6 7.4 %copy-start.16 = (bf16[2,64,1,128]{1,2,3,0:T(2,128)(2,1)S(1)}, bf16[2,64,1,128]{1,2,3,0:T(2,128)(2,1)}, u32[]{:S(2)}) copy-start(bf16[2,64,1,128]{1,2,3,0:T(2,128)(2,1)} %copy-done.15) | copy-start | bytes 98308
  296.6 7.4 %copy-start.19 = (bf16[34]{0:T(256)(128)(2,1)S(1)}, bf16[34]{0:T(256)(128)(2,1)}, u32[]{:S(2)}) copy-start(bf16[34]{0:T(256)(128)(2,1)} %copy-done.18) | copy-start | bytes 208
  307.5 5.8 %copy-start.24 = (pred[16,17]{0,1:T(8,128)(4,1)S(1)}, pred[16,17]{0,1:T(8,128)(4,1)}, u32[]{:S(2)}) copy-start(pred[16,17]{0,1:T(8,128)(4,1)} %constant.31) | copy-start | bytes 820
  310.1 10.1 %slice-start = ((s8[4456448]{0:T(1024)(128)(4,1)}), s8[4194304]{0:T(1024)(128)(4,1)S(1)}, s32[]{:S(2)}) async-start(s8[4456448]{0:T(1024)(128)(4,1)} %bitcast.55), calls=%async_computation.1 | async-start | bytes 8388608
  313.3 6.8 %slice-start.1 = ((s8[4456448]{0:T(1024)(128)(4,1)}), s8[262144]{0:T(1024)(128)(4,1)S(1)}, s32[]{:S(2)}) async-start(s8[4456448]{0:T(1024)(128)(4,1)} %bitcast.55), calls=%async_computation.2 | async-start | bytes 524288
  (12 other events, 26.8 us)
Sparse Core Ops, SparseCore 0:
  302.7 141.5 all-reduce.3
where the time goes:
time: 462 us; the launch traced here: 453 us
  blocking collectives  193 us (42%)
  waiting for transfers between devices  115 us (25%)
  local copies, waits for them, and re-layouts  54.1 us (12%)
  other arithmetic  34.7 us (8%)
  matrix products  24.1 us (5%)
  between operations  16.3 us (4%)
  starting transfers between devices  15.9 us (3%)
    psum x1, waiting for transfers between devices, on_device(): weight_grad = lax.psum(local_weight, ('lat', 'lon'))  113 us
    psum x1, blocking collectives, on_device(): lax.psum((jnp.sum(conv * full_ocean_mask, axis=(0, 2, 3)), local_count),...  66.6 us
    psum x1, blocking collectives, on_device(): lax.psum(jnp.sum(dev_inner * dev_inner * full_ocean_mask, axis=(0, 2, 3))...  63.6 us
    psum x1, blocking collectives, on_device(): lax.psum((jnp.sum(preactivation_gradient, axis=(0, 2, 3)), jnp.sum(preact...  63 us
    unnamed x62, local copies, waits for them, and re-layouts  27.2 us
    transpose x1, matrix products, kernel_grad(): return jnp.transpose(raw, (2, 3, 0, 1))  15.6 us
  transfers between devices with their start and end apart: 9, of which 2 were waited for; matrix products, arithmetic and copies ran while one was open for 14% of the time, Pallas kernels for 0%

commit v1 on v0

v1 whole, which is shorter than its diff:
```python
import jax
import jax.numpy as jnp
from jax import lax
from jax.experimental import pallas as pl
from jax.experimental.pallas import tpu as pltpu
from jax.sharding import PartitionSpec as P

BF = jnp.bfloat16
F32 = jnp.float32
MESH = pl.DeviceIdType.MESH
NT = (((1,), (1,)), ((), ()))


def peer_offsets():
    found = []
    for dx in range(4):
        for dy in range(4):
            for dz in range(4):
                for dc in range(2):
                    if dx or dy or dz or dc:
                        hops = sum(min(a, 4 - a) for a in (dx, dy, dz))
                        found.append((-hops, dx, dy, dz, dc))
    found.sort()
    return [t[1:] for t in found]


OFFSETS = peer_offsets()


def peer(lat, lon, offset):
    dx, dy, dz, dc = offset
    plat = lax.rem(lax.div(lat, 4) + dx, 4) * 4 + lax.rem(lat + dy, 4)
    plon = lax.rem(lax.div(lon, 2) + dz, 4) * 2 + lax.rem(lon + dc, 2)
    return plat, plon


def kernel(
    state, mask, weight, gain, bias, cot,
    act_out, sgrad_out, wgrad_out, gain_out, bias_out,
    xin, cin, aout, sout, xs, ds, cv, dp, ctm, actt, wf, wb, epx, epd, erx, erd,
    stat_src, stat_buf, grad_src, grad_buf, wsrc, wbuf, acc, wgat, cols, mrow,
    dma, hsx, hrx, hsd, hrd, gss, grs,
):
    lat = lax.axis_index("lat")
    lon = lax.axis_index("lon")
    me = lat * 8 + lon
    north, south = lax.rem(lat + 15, 16), lax.rem(lat + 1, 16)
    west, east = lax.rem(lon + 7, 8), lax.rem(lon + 1, 8)

    load_x = pltpu.make_async_copy(state, xin, dma.at[0])
    load_x.start()
    load_c = pltpu.make_async_copy(cot, cin, dma.at[1])
    load_c.start()
    barrier = pltpu.get_barrier_semaphore()
    for f in OFFSETS:
        pl.semaphore_signal(barrier, 1, device_id=peer(lat, lon, f), device_id_type=MESH)

    maskf = mask[...].astype(F32)
    mrow[...] = maskf
    mask_bf = maskf.astype(BF)
    n_local = 2.0 * jnp.sum(jnp.sum(maskf, axis=0, keepdims=True), axis=1, keepdims=True)

    taps = weight[...].reshape(576, 64)
    wt = jnp.transpose(taps.astype(F32), (1, 0)).astype(BF)
    zero = jnp.zeros((64, 192), BF)
    wf[0:64, :] = jnp.concatenate([wt, zero], axis=1)
    wf[64:128, :] = jnp.concatenate([zero, wt], axis=1)
    back = jnp.concatenate([weight[2 - t // 3, 2 - t % 3] for t in range(9)], axis=1)
    wb[0:64, :] = jnp.concatenate([back, zero], axis=1)
    wb[64:128, :] = jnp.concatenate([zero, back], axis=1)
    gb = jnp.concatenate([gain[...].reshape(1, 64), bias[...].reshape(1, 64)], axis=1)
    gg = jnp.concatenate([gain[...].reshape(1, 64), gain[...].reshape(1, 64)], axis=1)

    def column(row):
        return jnp.transpose(jnp.broadcast_to(row, (128, 128)), (1, 0))

    gbc = column(gb)
    cols[0:128, :] = gbc

    lane = lax.broadcasted_iota(jnp.int32, (64, 128), 1)

    def shifts_and_pack(buf, epack):
        packed = jnp.zeros((64, 128), BF)
        for b in range(2):
            half = pl.ds(b * 128, 128)
            for i in range(32):
                q = b * 32 + i
                base = (i + 1) * 192
                v = buf[base + 64:base + 128, half]
                buf[base:base + 64, half] = pltpu.roll(v, 1, 1)
                buf[base + 128:base + 192, half] = pltpu.roll(v, 127, 1)
                turned = pltpu.roll(v, (2 * q + 1) % 128, 1)
                packed = jnp.where(lax.div(lane, 2) == q, turned, packed)
        epack[...] = packed

    def halo_copies(buf, epack, erecv, ss, rs):
        row = lambda p: buf.at[pl.ds((p * 3 + 1) * 64, 64)]
        plan = [
            (row(1), row(33), (north, lon)),
            (row(32), row(0), (south, lon)),
            (epack, erecv.at[0], (lat, east)),
            (epack, erecv.at[1], (lat, west)),
            (epack, erecv.at[2], (south, east)),
            (epack, erecv.at[3], (south, west)),
            (epack, erecv.at[4], (north, east)),
            (epack, erecv.at[5], (north, west)),
        ]
        return [
            pltpu.make_async_remote_copy(
                src_ref=s, dst_ref=d, send_sem=ss.at[k], recv_sem=rs.at[k], device_id=t, device_id_type=MESH
            )
            for k, (s, d, t) in enumerate(plan)
        ]

    def insert(buf, p, b, joined, q):
        half = pl.ds(b * 128, 128)
        base = p * 192
        r = pltpu.roll(joined, (127 - 2 * q) % 128, 1)
        buf[base:base + 64, half] = jnp.where(lane == 0, r, buf[base:base + 64, half])
        buf[base + 128:base + 192, half] = jnp.where(lane == 127, r, buf[base + 128:base + 192, half])

    def join(left, right):
        return jnp.where(lax.rem(lane, 2) == 0, pltpu.roll(right, 127, 1), pltpu.roll(left, 1, 1))

    def finish_halo(buf, erecv):
        for p, keep in ((0, lat > 0), (33, lat < 15)):
            base = p * 192
            scale = jnp.where(keep, 1.0, 0.0).astype(F32)
            v = (buf[base + 64:base + 128, :].astype(F32) * scale).astype(BF)
            buf[base + 64:base + 128, :] = v
            for b in range(2):
                half = pl.ds(b * 128, 128)
                vb = v[:, b * 128:(b + 1) * 128]
                buf[base:base + 64, half] = pltpu.roll(vb, 1, 1)
                buf[base + 128:base + 192, half] = pltpu.roll(vb, 127, 1)
            left, right, i = (erecv[2], erecv[3], 31) if p == 0 else (erecv[4], erecv[5], 0)
            corner = (join(left, right).astype(F32) * scale).astype(BF)
            for b in range(2):
                insert(buf, p, b, corner, b * 32 + i)
        joined = join(erecv[0], erecv[1])
        for b in range(2):
            for i in range(32):
                insert(buf, i + 1, b, joined, b * 32 + i)

    def exchange(src, buf, sem):
        for f in OFFSETS:
            pltpu.make_async_remote_copy(
                src_ref=src, dst_ref=buf.at[me], send_sem=gss.at[sem], recv_sem=grs.at[sem],
                device_id=peer(lat, lon, f), device_id_type=MESH,
            ).start()

    def exchange_wait(buf, sem):
        pltpu.make_async_copy(buf.at[pl.ds(0, 127)], buf.at[pl.ds(0, 127)], grs.at[sem]).wait()
        pltpu.make_async_copy(buf.at[pl.ds(0, 127)], buf.at[pl.ds(0, 127)], gss.at[sem]).wait()

    load_x.wait()
    for b in range(2):
        t = jnp.transpose(xin[b] * mask_bf[None], (1, 0, 2))
        for i in range(32):
            xs[(i + 1) * 192 + 64:(i + 1) * 192 + 128, b * 128:(b + 1) * 128] = t[i]
    shifts_and_pack(xs, epx)

    pl.semaphore_wait(barrier, 127)
    halo_x = halo_copies(xs, epx, erx, hsx, hrx)
    for c in halo_x:
        c.start()
    load_c.wait()
    for b in range(2):
        t = jnp.transpose(cin[b] * mask_bf[None], (1, 0, 2))
        for i in range(32):
            ctm[i * 64:(i + 1) * 64, b * 128:(b + 1) * 128] = t[i]
    for c in halo_x:
        c.wait()
    finish_halo(xs, erx)

    first = jnp.zeros((64, 128), F32)
    for p in range(16):
        r = jnp.dot(wf[...], xs[p * 384:p * 384 + 768, :], preferred_element_type=F32)
        cv[p * 128:(p + 1) * 128, :] = r
        for h in range(2):
            m = mrow[2 * p + h:2 * p + h + 1, :]
            first = first + (r[h * 64:(h + 1) * 64, :128] + r[h * 64:(h + 1) * 64, 128:]) * m
    mean_here = jnp.sum(first, axis=1, keepdims=True) / jnp.maximum(n_local, 1.0)
    mean_here = jnp.broadcast_to(mean_here, (64, 128))
    second = jnp.zeros((64, 128), F32)
    for i in range(32):
        m = mrow[i:i + 1, :]
        for b in range(2):
            d = cv[i * 64:(i + 1) * 64, b * 128:(b + 1) * 128] - mean_here
            second = second + d * d * m
    row = jnp.sum(jnp.transpose(jnp.concatenate([first, second], axis=0), (1, 0)), axis=0, keepdims=True)
    stat_src[...] = jnp.concatenate([row, jnp.broadcast_to(n_local, (1, 128))], axis=0)
    exchange(stat_src, stat_buf, 0)
    stat_buf[me] = stat_src[...]
    exchange_wait(stat_buf, 0)
    sums = stat_buf[:, 0, :]
    counts = stat_buf[:, 1, :]
    total = jnp.sum(sums, axis=0, keepdims=True)
    count = jnp.maximum(jnp.sum(counts, axis=0, keepdims=True), 1.0)
    mean = total / count
    apart = sums / jnp.maximum(counts, 1.0) - mean
    between = jnp.sum(apart * apart * counts, axis=0, keepdims=True)
    var = (total + pltpu.roll(between, 64, 1)) / count
    low = lax.broadcasted_iota(jnp.int32, (1, 128), 1) < 64
    mi = column(jnp.where(low, mean, lax.rsqrt(var + 1e-05)))
    cols[128:256, :] = mi

    mean_c, inv_c, gain_c, bias_c = cols[128:192, :], cols[192:256, :], cols[0:64, :], cols[64:128, :]
    gsum = jnp.zeros((64, 128), F32)
    bsum = jnp.zeros((64, 128), F32)
    for i in range(32):
        for b in range(2):
            at = (pl.ds(i * 64, 64), pl.ds(b * 128, 128))
            xhat = (cv[at] - mean_c) * inv_c
            pre = gain_c * xhat + bias_c
            s = 1.0 / (1.0 + jnp.exp(-pre))
            actt[at] = (pre * s).astype(BF)
            d = ctm[at].astype(F32) * (s * (1.0 + pre * (1.0 - s)))
            dp[at] = d
            bsum = bsum + d
            gsum = gsum + d * xhat
    grad_src[...] = jnp.sum(jnp.transpose(jnp.concatenate([bsum, gsum], axis=0), (1, 0)), axis=0, keepdims=True)
    exchange(grad_src, grad_buf, 1)
    grad_buf[me] = grad_src[...]

    def native(src, b):
        t = src[:, b * 128:(b + 1) * 128].reshape(32, 64, 128)
        return jnp.transpose(t, (1, 0, 2)) * mask_bf[None]

    for b in range(2):
        aout[b] = native(actt, b)
    save_a = pltpu.make_async_copy(aout, act_out, dma.at[0])
    save_a.start()

    exchange_wait(grad_buf, 1)
    gtot = jnp.sum(grad_buf[:, 0, :], axis=0, keepdims=True)
    bias_out[...] = gtot[0, :64]
    gain_out[...] = pltpu.roll(gtot, 64, 1)[0, :64]
    sc = column(gg * gtot / count)
    cols[256:384, :] = sc
    sf_c, sg_c = cols[256:320, :], cols[320:384, :]

    for i in range(32):
        m = mrow[i:i + 1, :]
        for b in range(2):
            at = (pl.ds(i * 64, 64), pl.ds(b * 128, 128))
            xhat = (cv[at] - mean_c) * inv_c
            d = m * inv_c * (gain_c * dp[at] - sf_c - xhat * sg_c)
            ds[(i + 1) * 192 + 64:(i + 1) * 192 + 128, b * 128:(b + 1) * 128] = d.astype(BF)
    shifts_and_pack(ds, epd)
    halo_d = halo_copies(ds, epd, erd, hsd, hrd)
    for c in halo_d:
        c.start()

    for p in range(8):
        right = jnp.concatenate(
            [ds[(4 * p + k + 1) * 192 + 64:(4 * p + k + 1) * 192 + 128, :] for k in range(4)], axis=0
        )
        part = lax.dot_general(xs[p * 768:p * 768 + 1152, :], right, NT, preferred_element_type=F32)
        if p == 0:
            acc[...] = part
        else:
            acc[...] += part
    here = []
    for ky in range(3):
        v = acc[ky * 192:(ky + 1) * 192, 0:64]
        for k in range(1, 4):
            v = v + acc[(ky + k) * 192:(ky + k + 1) * 192, k * 64:(k + 1) * 64]
        here.append(v)
    here = jnp.concatenate(here, axis=0)
    wsrc[...] = jnp.concatenate([here[:288], here[288:]], axis=1).reshape(72, 4, 128)

    def owner(la, lo):
        half = lax.rem(la, 2)
        return jnp.logical_or(half == 0, lo == 0), lax.div(la, 2) * 9 + half * 8 + lo

    own, mine = owner(lat, lon)
    for f in OFFSETS:
        la, lo = peer(lat, lon, f)
        owns, block = owner(la, lo)

        @pl.when(owns)
        def _():
            pltpu.make_async_remote_copy(
                src_ref=wsrc.at[block], dst_ref=wbuf.at[me], send_sem=gss.at[2], recv_sem=grs.at[2],
                device_id=(la, lo), device_id_type=MESH,
            ).start()

    @pl.when(own)
    def _():
        wbuf[me] = wsrc[mine]

    for c in halo_d:
        c.wait()
    finish_halo(ds, erd)
    for p in range(16):
        r = jnp.dot(wb[...], ds[p * 384:p * 384 + 768, :], preferred_element_type=F32)
        actt[p * 128:(p + 1) * 128, :] = r.astype(BF)
    for b in range(2):
        sout[b] = native(actt, b)
    save_s = pltpu.make_async_copy(sout, sgrad_out, dma.at[1])
    save_s.start()

    @pl.when(own)
    def _():
        pltpu.make_async_copy(wbuf.at[pl.ds(0, 127)], wbuf.at[pl.ds(0, 127)], grs.at[2]).wait()
        pltpu.make_async_copy(wsrc.at[pl.ds(0, 71)], wsrc.at[pl.ds(0, 71)], gss.at[2]).wait()
        wgat[mine] = jnp.sum(wbuf[...], axis=0)
        for f in OFFSETS:
            pltpu.make_async_remote_copy(
                src_ref=wgat.at[mine], dst_ref=wgat.at[mine], send_sem=gss.at[3], recv_sem=grs.at[3],
                device_id=peer(lat, lon, f), device_id_type=MESH,
            ).start()
        pltpu.make_async_copy(wgat.at[pl.ds(0, 71)], wgat.at[pl.ds(0, 71)], grs.at[3]).wait()
        pltpu.make_async_copy(wbuf.at[pl.ds(0, 127)], wbuf.at[pl.ds(0, 127)], gss.at[3]).wait()

    @pl.when(jnp.logical_not(own))
    def _():
        pltpu.make_async_copy(wsrc, wsrc, gss.at[2]).wait()
        pltpu.make_async_copy(wgat, wgat, grs.at[3]).wait()

    w = wgat[...].reshape(288, 128)
    wgrad_out[...] = jnp.concatenate([w[:, :64], w[:, 64:]], axis=0).reshape(3, 3, 64, 64)
    save_a.wait()
    save_s.wait()


def on_device(state, land_mask, conv_weight, norm_gain, batchnorm_bias, cotangent):
    vm = pl.BlockSpec(memory_space=pltpu.VMEM)
    anywhere = pl.BlockSpec(memory_space=pl.ANY)
    S = jax.ShapeDtypeStruct
    big = (2, 64, 32, 128)
    V = pltpu.VMEM
    return pl.pallas_call(
        kernel,
        out_shape=[S(big, BF), S(big, BF), S((3, 3, 64, 64), F32), S((64,), F32), S((64,), F32)],
        in_specs=[anywhere, vm, vm, vm, vm, anywhere],
        out_specs=[anywhere, anywhere, vm, vm, vm],
        scratch_shapes=[
            V(big, BF), V(big, BF), V(big, BF), V(big, BF),
            V((34 * 192, 256), BF), V((34 * 192, 256), BF),
            V((2048, 256), F32), V((2048, 256), F32), V((2048, 256), BF), V((2048, 256), BF),
            V((128, 768), BF), V((128, 768), BF),
            V((64, 128), BF), V((64, 128), BF), V((6, 64, 128), BF), V((6, 64, 128), BF),
            V((2, 128), F32), V((128, 2, 128), F32), V((1, 128), F32), V((128, 1, 128), F32),
            V((72, 4, 128), F32), V((128, 4, 128), F32), V((1152, 256), F32), V((72, 4, 128), F32),
            V((384, 128), F32), V((32, 128), F32),
            pltpu.SemaphoreType.DMA((2,)),
            pltpu.SemaphoreType.DMA((8,)), pltpu.SemaphoreType.DMA((8,)),
            pltpu.SemaphoreType.DMA((8,)), pltpu.SemaphoreType.DMA((8,)),
            pltpu.SemaphoreType.DMA((4,)), pltpu.SemaphoreType.DMA((4,)),
        ],
        compiler_params=pltpu.CompilerParams(
            collective_id=0, has_side_effects=True, vmem_limit_bytes=48 * 2**20
        ),
    )(state, land_mask, conv_weight, norm_gain, batchnorm_bias, cotangent)


def solution(mesh):
    return jax.shard_map(
        on_device,
        mesh=mesh,
        in_specs=(
            P(None, None, "lat", "lon"),
            P("lat", "lon"),
            P(),
            P(),
            P(),
            P(None, None, "lat", "lon"),
        ),
        out_specs=(P(None, None, "lat", "lon"), P(None, None, "lat", "lon"), P(), P(), P()),
        check_vma=False,
    )
```

time: 462 us -> 57.7 us (0.12); the launches traced: 453 us -> 57.5 us
  blocking collectives: 193 us -> 0 us
  waiting for transfers between devices: 115 us -> 0 us
  Pallas kernels: 0 us -> 47.7 us
  local copies, waits for them, and re-layouts: 54.1 us -> 9.06 us
  other arithmetic: 34.7 us -> 0 us
  matrix products: 24.1 us -> 0 us
  starting transfers between devices: 15.9 us -> 0 us
  between operations: 16.3 us -> 0.66 us
    psum x3 -> x0, blocking collectives: 193 us -> none  [the longest x1 66.6 us: on_device(): lax.psum((jnp.sum(conv * full_ocean_mask, axis=(0, 2, 3)), local_count),...]
    psum x1 -> x0, waiting for transfers between devices: 113 us -> none  [on_device(): weight_grad = lax.psum(local_weight, ('lat', 'lon'))]
    pallas_call x0 -> x1, Pallas kernels: none -> 47.7 us  [on_device(): pl.pallas_call(kernel, out_shape=[S(big, BF), S(big, BF), S((3, 3, 64, 64...]
    unnamed x62 -> x17, local copies, waits for them, and re-layouts: 27.2 us -> 9.06 us
    mul x8 -> x0, other arithmetic: 18.1 us -> none  [the longest x1 5.48 us: on_device(): normalized_state * shifted_second]
    mul x7 -> x0, local copies, waits for them, and re-layouts: 16.4 us -> none  [the longest x1 5.92 us: on_device(): preactivation * sigmoid_pre * full_ocean_mask]
    ppermute x8 -> x0, starting transfers between devices: 15.9 us -> none  [the longest x4 8.32 us: padded_2(): lax.ppermute(head, axis, [((i + 1) % count, i) for i in range(count)])]
    transpose x1 -> x0, matrix products: 15.6 us -> none  [kernel_grad(): return jnp.transpose(raw, (2, 3, 0, 1))]
  transfers between devices with their start and end apart: 9 -> 0, of which waited for: 2 -> 0; matrix products, arithmetic and copies ran while one was open for 14% -> 0% of each run, Pallas kernels for 0% -> 0%
where the time goes in v1:
time: 57.7 us; the launch traced here: 57.5 us
  Pallas kernels  47.7 us (83%)
  local copies, waits for them, and re-layouts  9.06 us (16%)
  between operations  0.66 us (1%)
    pallas_call x1, Pallas kernels, on_device(): pl.pallas_call(kernel, out_shape=[S(big, BF), S(big, BF), S((3, 3, 64, 64...  47.7 us
    unnamed x17, local copies, waits for them, and re-layouts  9.06 us

profile of v1, /device:TPU:1, one launch (start us, length us, event | category | flops | bytes accessed | tf_op | source)
XLA Modules:
  0.0 57.5 jit_solution(8314080712184449588)
XLA Ops:
  0.6 0.0 copy-start
  0.6 1.2 %copy-done = bf16[2,64,32,128]{3,2,1,0:T(8,128)(2,1)S(1)} copy-done((bf16[2,64,32,128]{3,2,1,0:T(8,128)(2,1)S(1)}, bf16[2,64,32,128]{3,2,1,0:T(8,128)(2,1)}, u32[]{:S(2)}) %copy-start) | copy-done | bytes 1048600
  1.9 0.0 copy-start.1
  1.9 1.2 %copy-done.1 = bf16[2,64,32,128]{3,2,1,0:T(8,128)(2,1)S(1)} copy-done((bf16[2,64,32,128]{3,2,1,0:T(8,128)(2,1)S(1)}, bf16[2,64,32,128]{3,2,1,0:T(8,128)(2,1)}, u32[]{:S(2)}) %copy-start.1) | copy-done | bytes 1048600
  3.1 0.0 copy-start.2
  3.1 0.9 %copy-done.2 = bf16[3,3,64,64]{3,2,1,0:T(8,128)(2,1)S(1)} copy-done((bf16[3,3,64,64]{3,2,1,0:T(8,128)(2,1)S(1)}, bf16[3,3,64,64]{3,2,1,0:T(8,128)(2,1)}, u32[]{:S(2)}) %copy-start.2) | copy-done | bytes 73752
  4.0 0.0 copy-start.3
  4.0 0.7 %copy-done.3 = s32[32,128]{1,0:T(8,128)S(1)} copy-done((s32[32,128]{1,0:T(8,128)S(1)}, s32[32,128]{1,0:T(8,128)}, u32[]{:S(2)}) %copy-start.3) | copy-done | bytes 16408
  4.7 0.0 copy-start.4
  4.7 0.7 %copy-done.4 = f32[64]{0:T(128)S(1)} copy-done((f32[64]{0:T(128)S(1)}, f32[64]{0:T(128)}, u32[]{:S(2)}) %copy-start.4) | copy-done | bytes 280
  5.4 0.0 copy-start.5
  5.4 0.7 %copy-done.5 = f32[64]{0:T(128)S(1)} copy-done((f32[64]{0:T(128)S(1)}, f32[64]{0:T(128)}, u32[]{:S(2)}) %copy-start.5) | copy-done | bytes 280
  6.0 47.7 %shard_map.101 = (bf16[2,64,32,128]{3,2,1,0:T(8,128)(2,1)S(1)}, bf16[2,64,32,128]{3,2,1,0:T(8,128)(2,1)S(1)}, f32[3,3,64,64]{3,2,1,0:T(8,128)S(1)}, f32[64]{0:T(128)S(1)}, f32[64]{0:T(128)S(1)}) custom-call(bf16[2,64,32,128]{3,2,1,0:T(8,128)(2,1)S(1)} %copy-done, s32[32,128]{1,0:T(8,128)S(1)} %copy-done.3, bf16[3,3,64,64]{3,2,1,0:T(8,128)(2,1)S(1)} %copy-done.2, ...), custom_call_target="tpu_custom_call" | custom-call | tf_op jit(solution)/shard_map/pallas_call | solution.py:334
  53.8 1.0 %copy.16 = bf16[2,64,32,128]{3,2,1,0:T(8,128)(2,1)} copy(bf16[2,64,32,128]{3,2,1,0:T(8,128)(2,1)S(1)} %get-tuple-element.10) | data formatting | bytes 2097152
  54.7 1.0 %copy.17 = bf16[2,64,32,128]{3,2,1,0:T(8,128)(2,1)} copy(bf16[2,64,32,128]{3,2,1,0:T(8,128)(2,1)S(1)} %get-tuple-element.11) | data formatting | bytes 2097152
  55.7 0.7 %copy.18 = f32[3,3,64,64]{3,2,1,0:T(8,128)} copy(f32[3,3,64,64]{3,2,1,0:T(8,128)S(1)} %get-tuple-element.12) | data formatting | bytes 294912
  56.4 0.5 copy.19
  56.9 0.5 copy.20
Async XLA Ops:
  0.6 1.2 %copy-start = (bf16[2,64,32,128]{3,2,1,0:T(8,128)(2,1)S(1)}, bf16[2,64,32,128]{3,2,1,0:T(8,128)(2,1)}, u32[]{:S(2)}) copy-start(bf16[2,64,32,128]{3,2,1,0:T(8,128)(2,1)} %state.1) | copy-start | bytes 3145732
  1.9 1.2 %copy-start.1 = (bf16[2,64,32,128]{3,2,1,0:T(8,128)(2,1)S(1)}, bf16[2,64,32,128]{3,2,1,0:T(8,128)(2,1)}, u32[]{:S(2)}) copy-start(bf16[2,64,32,128]{3,2,1,0:T(8,128)(2,1)} %cot.1) | copy-start | bytes 3145732
  3.1 0.9 %copy-start.2 = (bf16[3,3,64,64]{3,2,1,0:T(8,128)(2,1)S(1)}, bf16[3,3,64,64]{3,2,1,0:T(8,128)(2,1)}, u32[]{:S(2)}) copy-start(bf16[3,3,64,64]{3,2,1,0:T(8,128)(2,1)} %weight.1) | copy-start | bytes 221188
  4.0 0.7 %copy-start.3 = (s32[32,128]{1,0:T(8,128)S(1)}, s32[32,128]{1,0:T(8,128)}, u32[]{:S(2)}) copy-start(s32[32,128]{1,0:T(8,128)} %mask.1) | copy-start | bytes 49156
  4.7 0.7 %copy-start.4 = (f32[64]{0:T(128)S(1)}, f32[64]{0:T(128)}, u32[]{:S(2)}) copy-start(f32[64]{0:T(128)} %gain.1) | copy-start | bytes 772
  5.4 0.7 %copy-start.5 = (f32[64]{0:T(128)S(1)}, f32[64]{0:T(128)}, u32[]{:S(2)}) copy-start(f32[64]{0:T(128)} %bias.1) | copy-start | bytes 772

commit v2 on v1

--- a/solution.py
+++ b/solution.py
@@ -35,9 +35,9 @@
 
 
 def kernel(
-    state, mask, weight, gain, bias, cot,
-    act_out, sgrad_out, wgrad_out, gain_out, bias_out,
-    xin, cin, aout, sout, xs, ds, cv, dp, ctm, actt, wf, wb, epx, epd, erx, erd,
+    state, mask_hbm, weight_hbm, gain_hbm, bias_hbm, cot,
+    aout, sout, wgrad_out, gain_out, bias_out,
+    xin, cin, mask, weight, gain, bias, xs, ds, cv, dp, ctm, actt, wf, wb, epx, epd, erx, erd,
     stat_src, stat_buf, grad_src, grad_buf, wsrc, wbuf, acc, wgat, cols, mrow,
     dma, hsx, hrx, hsd, hrd, gss, grs,
 ):
@@ -47,14 +47,20 @@
     north, south = lax.rem(lat + 15, 16), lax.rem(lat + 1, 16)
     west, east = lax.rem(lon + 7, 8), lax.rem(lon + 1, 8)
 
-    load_x = pltpu.make_async_copy(state, xin, dma.at[0])
-    load_x.start()
-    load_c = pltpu.make_async_copy(cot, cin, dma.at[1])
-    load_c.start()
+    loads = [
+        pltpu.make_async_copy(s, d, dma.at[k])
+        for k, (s, d) in enumerate(
+            [(state, xin), (mask_hbm, mask), (weight_hbm, weight), (gain_hbm, gain), (bias_hbm, bias), (cot, cin)]
+        )
+    ]
+    for c in loads:
+        c.start()
     barrier = pltpu.get_barrier_semaphore()
     for f in OFFSETS:
         pl.semaphore_signal(barrier, 1, device_id=peer(lat, lon, f), device_id_type=MESH)
 
+    for c in loads[1:5]:
+        c.wait()
     maskf = mask[...].astype(F32)
     mrow[...] = maskf
     mask_bf = maskf.astype(BF)
@@ -153,7 +159,7 @@
         pltpu.make_async_copy(buf.at[pl.ds(0, 127)], buf.at[pl.ds(0, 127)], grs.at[sem]).wait()
         pltpu.make_async_copy(buf.at[pl.ds(0, 127)], buf.at[pl.ds(0, 127)], gss.at[sem]).wait()
 
-    load_x.wait()
+    loads[0].wait()
     for b in range(2):
         t = jnp.transpose(xin[b] * mask_bf[None], (1, 0, 2))
         for i in range(32):
@@ -164,7 +170,7 @@
     halo_x = halo_copies(xs, epx, erx, hsx, hrx)
     for c in halo_x:
         c.start()
-    load_c.wait()
+    loads[5].wait()
     for b in range(2):
         t = jnp.transpose(cin[b] * mask_bf[None], (1, 0, 2))
         for i in range(32):
@@ -229,8 +235,6 @@
 
     for b in range(2):
         aout[b] = native(actt, b)
-    save_a = pltpu.make_async_copy(aout, act_out, dma.at[0])
-    save_a.start()
 
     exchange_wait(grad_buf, 1)
     gtot = jnp.sum(grad_buf[:, 0, :], axis=0, keepdims=True)
@@ -247,11 +251,6 @@
             xhat = (cv[at] - mean_c) * inv_c
             d = m * inv_c * (gain_c * dp[at] - sf_c - xhat * sg_c)
             ds[(i + 1) * 192 + 64:(i + 1) * 192 + 128, b * 128:(b + 1) * 128] = d.astype(BF)
-    shifts_and_pack(ds, epd)
-    halo_d = halo_copies(ds, epd, erd, hsd, hrd)
-    for c in halo_d:
-        c.start()
-
     for p in range(8):
         right = jnp.concatenate(
             [ds[(4 * p + k + 1) * 192 + 64:(4 * p + k + 1) * 192 + 128, :] for k in range(4)], axis=0
@@ -290,27 +289,32 @@
     def _():
         wbuf[me] = wsrc[mine]
 
+    shifts_and_pack(ds, epd)
+    halo_d = halo_copies(ds, epd, erd, hsd, hrd)
+    for c in halo_d:
+        c.start()
     for c in halo_d:
         c.wait()
     finish_halo(ds, erd)
     for p in range(16):
         r = jnp.dot(wb[...], ds[p * 384:p * 384 + 768, :], preferred_element_type=F32)
         actt[p * 128:(p + 1) * 128, :] = r.astype(BF)
-    for b in range(2):
-        sout[b] = native(actt, b)
-    save_s = pltpu.make_async_copy(sout, sgrad_out, dma.at[1])
-    save_s.start()
-
     @pl.when(own)
     def _():
         pltpu.make_async_copy(wbuf.at[pl.ds(0, 127)], wbuf.at[pl.ds(0, 127)], grs.at[2]).wait()
-        pltpu.make_async_copy(wsrc.at[pl.ds(0, 71)], wsrc.at[pl.ds(0, 71)], gss.at[2]).wait()
         wgat[mine] = jnp.sum(wbuf[...], axis=0)
         for f in OFFSETS:
             pltpu.make_async_remote_copy(
                 src_ref=wgat.at[mine], dst_ref=wgat.at[mine], send_sem=gss.at[3], recv_sem=grs.at[3],
                 device_id=peer(lat, lon, f), device_id_type=MESH,
             ).start()
+
+    for b in range(2):
+        sout[b] = native(actt, b)
+
+    @pl.when(own)
+    def _():
+        pltpu.make_async_copy(wsrc.at[pl.ds(0, 71)], wsrc.at[pl.ds(0, 71)], gss.at[2]).wait()
         pltpu.make_async_copy(wgat.at[pl.ds(0, 71)], wgat.at[pl.ds(0, 71)], grs.at[3]).wait()
         pltpu.make_async_copy(wbuf.at[pl.ds(0, 127)], wbuf.at[pl.ds(0, 127)], gss.at[3]).wait()
 
@@ -321,23 +325,31 @@
 
     w = wgat[...].reshape(288, 128)
     wgrad_out[...] = jnp.concatenate([w[:, :64], w[:, 64:]], axis=0).reshape(3, 3, 64, 64)
-    save_a.wait()
-    save_s.wait()
+
+
+def store(*refs):
+    copies = [pltpu.make_async_copy(refs[k], refs[k + 5], refs[10].at[k]) for k in range(5)]
+    for c in copies:
+        c.start()
+    for c in copies:
+        c.wait()
 
 
 def on_device(state, land_mask, conv_weight, norm_gain, batchnorm_bias, cotangent):
     vm = pl.BlockSpec(memory_space=pltpu.VMEM)
+    hbm = pl.BlockSpec(memory_space=pltpu.HBM)
     anywhere = pl.BlockSpec(memory_space=pl.ANY)
     S = jax.ShapeDtypeStruct
     big = (2, 64, 32, 128)
+    outs = [S(big, BF), S(big, BF), S((3, 3, 64, 64), F32), S((64,), F32), S((64,), F32)]
     V = pltpu.VMEM
-    return pl.pallas_call(
+    made = pl.pallas_call(
         kernel,
-        out_shape=[S(big, BF), S(big, BF), S((3, 3, 64, 64), F32), S((64,), F32), S((64,), F32)],
-        in_specs=[anywhere, vm, vm, vm, vm, anywhere],
-        out_specs=[anywhere, anywhere, vm, vm, vm],
+        out_shape=outs,
+        in_specs=[hbm] * 6,
+        out_specs=[vm] * 5,
         scratch_shapes=[
-            V(big, BF), V(big, BF), V(big, BF), V(big, BF),
+            V(big, BF), V(big, BF), V((32, 128), jnp.int32), V((3, 3, 64, 64), BF), V((64,), F32), V((64,), F32),
             V((34 * 192, 256), BF), V((34 * 192, 256), BF),
             V((2048, 256), F32), V((2048, 256), F32), V((2048, 256), BF), V((2048, 256), BF),
             V((128, 768), BF), V((128, 768), BF),
@@ -345,15 +357,22 @@
             V((2, 128), F32), V((128, 2, 128), F32), V((1, 128), F32), V((128, 1, 128), F32),
             V((72, 4, 128), F32), V((128, 4, 128), F32), V((1152, 256), F32), V((72, 4, 128), F32),
             V((384, 128), F32), V((32, 128), F32),
-            pltpu.SemaphoreType.DMA((2,)),
+            pltpu.SemaphoreType.DMA((6,)),
             pltpu.SemaphoreType.DMA((8,)), pltpu.SemaphoreType.DMA((8,)),
             pltpu.SemaphoreType.DMA((8,)), pltpu.SemaphoreType.DMA((8,)),
             pltpu.SemaphoreType.DMA((4,)), pltpu.SemaphoreType.DMA((4,)),
         ],
         compiler_params=pltpu.CompilerParams(
-            collective_id=0, has_side_effects=True, vmem_limit_bytes=48 * 2**20
+            collective_id=0, has_side_effects=True, vmem_limit_bytes=40 * 2**20
         ),
-    )(state, land_mask, conv_weight, norm_gain, batchnorm_bias, cotangent)
+    )(*[pltpu.with_memory_space_constraint(a, pltpu.HBM) for a in (state, land_mask, conv_weight, norm_gain, batchnorm_bias, cotangent)])
+    return pl.pallas_call(
+        store,
+        out_shape=outs,
+        in_specs=[vm] * 5,
+        out_specs=[anywhere] * 5,
+        scratch_shapes=[pltpu.SemaphoreType.DMA((5,))],
+    )(*[pltpu.with_memory_space_constraint(a, pltpu.VMEM) for a in made])
 
 
 def solution(mesh):

time: 57.7 us -> 51.3 us (0.89)
  local copies, waits for them, and re-layouts: 9.06 us -> 0 us
  Pallas kernels: 47.7 us -> 50.3 us
    unnamed x17 -> x0, local copies, waits for them, and re-layouts: 9.06 us -> none
    pallas_call x1 -> x2, Pallas kernels: 47.7 us -> 50.3 us  [the longest x1 48.9 us: on_device(): pl.pallas_call(kernel, out_shape=outs, in_specs=[hbm] * 6, out_specs=[vm]...]
where the time goes in v2:
time: 51.3 us; the launch traced here: 51.1 us
  Pallas kernels  50.3 us (98%)
  between operations  0.8 us (2%)
    pallas_call x1, Pallas kernels, on_device(): pl.pallas_call(kernel, out_shape=outs, in_specs=[hbm] * 6, out_specs=[vm]...  48.9 us
    pallas_call x1, Pallas kernels, on_device(): pl.pallas_call(store, out_shape=outs, in_specs=[vm] * 5, out_specs=[anywh...  1.45 us

profile of v2, /device:TPU:1, one launch (start us, length us, event | category | flops | bytes accessed | tf_op | source)
XLA Modules:
  0.0 51.1 jit_solution(12822600873278280733)
XLA Ops:
  0.6 48.9 %shard_map.101 = (bf16[2,64,32,128]{3,2,1,0:T(8,128)(2,1)S(1)}, bf16[2,64,32,128]{3,2,1,0:T(8,128)(2,1)S(1)}, f32[3,3,64,64]{3,2,1,0:T(8,128)S(1)}, f32[64]{0:T(128)S(1)}, f32[64]{0:T(128)S(1)}) custom-call(bf16[2,64,32,128]{3,2,1,0:T(8,128)(2,1)} %state.1, s32[32,128]{1,0:T(8,128)} %mask_hbm.1, bf16[3,3,64,64]{3,2,1,0:T(8,128)(2,1)} %weight_hbm.1, ...), custom_call_target="tpu_custom_call" | custom-call | tf_op jit(solution)/shard_map/pallas_call | solution.py:346
  49.5 1.5 %shard_map.102 = (bf16[2,64,32,128]{3,2,1,0:T(8,128)(2,1)}, bf16[2,64,32,128]{3,2,1,0:T(8,128)(2,1)}, f32[3,3,64,64]{3,2,1,0:T(8,128)}, f32[64]{0:T(128)}, f32[64]{0:T(128)}) custom-call(bf16[2,64,32,128]{3,2,1,0:T(8,128)(2,1)S(1)} %get-tuple-element.10.refs_0_, bf16[2,64,32,128]{3,2,1,0:T(8,128)(2,1)S(1)} %get-tuple-element.11.refs_1_, ...), custom_call_target="tpu_custom_call" | custom-call | tf_op jit(solution)/shard_map/pallas_call | solution.py:369

commit v3 on v2

--- a/solution.py
+++ b/solution.py
@@ -25,13 +25,9 @@
 
 
 OFFSETS = peer_offsets()
-
-
-def peer(lat, lon, offset):
-    dx, dy, dz, dc = offset
-    plat = lax.rem(lax.div(lat, 4) + dx, 4) * 4 + lax.rem(lat + dy, 4)
-    plon = lax.rem(lax.div(lon, 2) + dz, 4) * 2 + lax.rem(lon + dc, 2)
-    return plat, plon
+FAR_XY = [(2, 2), (2, 1), (2, 3), (1, 2), (3, 2), (2, 0), (0, 2), (1, 1), (1, 3), (3, 1), (3, 3), (1, 0), (3, 0), (0, 1), (0, 3), (0, 0)]
+GREETED = [(a, 0) for a in (10, 6, 2, 14, 9, 11, 5, 7, 8, 1, 3, 13, 15, 4, 12)]
+GREETED = [(1, 1), (1, 7), (15, 1), (15, 7)] + GREETED + [(0, b) for b in (4, 5, 3, 2, 6, 1, 7)]
 
 
 def kernel(
@@ -39,11 +35,21 @@
     aout, sout, wgrad_out, gain_out, bias_out,
     xin, cin, mask, weight, gain, bias, xs, ds, cv, dp, ctm, actt, wf, wb, epx, epd, erx, erd,
     stat_src, stat_buf, grad_src, grad_buf, wsrc, wbuf, acc, wgat, cols, mrow,
-    dma, hsx, hrx, hsd, hrd, gss, grs,
+    dma, hsx, hrx, hsd, hrd, gss, grs, all_here,
 ):
     lat = lax.axis_index("lat")
     lon = lax.axis_index("lon")
     me = lat * 8 + lon
+    x, y, z, core = lax.div(lat, 4), lax.rem(lat, 4), lax.div(lon, 2), lax.rem(lon, 2)
+    xs_at = [lax.rem(x + d, 4) for d in range(4)]
+    ys_at = [lax.rem(y + d, 4) for d in range(4)]
+    lats = [[xs_at[dx] * 4 + ys_at[dy] for dy in range(4)] for dx in range(4)]
+    lons = [[lax.rem(z + d, 4) * 2 + lax.rem(core + c, 2) for c in range(2)] for d in range(4)]
+
+    def peer(offset):
+        dx, dy, dz, dc = offset
+        return lats[dx][dy], lons[dz][dc]
+
     north, south = lax.rem(lat + 15, 16), lax.rem(lat + 1, 16)
     west, east = lax.rem(lon + 7, 8), lax.rem(lon + 1, 8)
 
@@ -56,8 +62,9 @@
     for c in loads:
         c.start()
     barrier = pltpu.get_barrier_semaphore()
-    for f in OFFSETS:
-        pl.semaphore_signal(barrier, 1, device_id=peer(lat, lon, f), device_id_type=MESH)
+    for a, b in GREETED:
+        there = (lax.rem(lat + a, 16), lax.rem(lon + b, 8))
+        pl.semaphore_signal(barrier, 1, device_id=there, device_id_type=MESH)
 
     for c in loads[1:5]:
         c.wait()
@@ -152,7 +159,7 @@
         for f in OFFSETS:
             pltpu.make_async_remote_copy(
                 src_ref=src, dst_ref=buf.at[me], send_sem=gss.at[sem], recv_sem=grs.at[sem],
-                device_id=peer(lat, lon, f), device_id_type=MESH,
+                device_id=peer(f), device_id_type=MESH,
             ).start()
 
     def exchange_wait(buf, sem):
@@ -166,10 +173,13 @@
             xs[(i + 1) * 192 + 64:(i + 1) * 192 + 128, b * 128:(b + 1) * 128] = t[i]
     shifts_and_pack(xs, epx)
 
-    pl.semaphore_wait(barrier, 127)
+    pl.semaphore_wait(barrier, len(GREETED))
     halo_x = halo_copies(xs, epx, erx, hsx, hrx)
     for c in halo_x:
         c.start()
+    for a, b in GREETED:
+        if a and not b:
+            pl.semaphore_signal(all_here, 1, device_id=(lax.rem(lat + a, 16), lon), device_id_type=MESH)
     loads[5].wait()
     for b in range(2):
         t = jnp.transpose(cin[b] * mask_bf[None], (1, 0, 2))
@@ -196,6 +206,7 @@
             second = second + d * d * m
     row = jnp.sum(jnp.transpose(jnp.concatenate([first, second], axis=0), (1, 0)), axis=0, keepdims=True)
     stat_src[...] = jnp.concatenate([row, jnp.broadcast_to(n_local, (1, 128))], axis=0)
+    pl.semaphore_wait(all_here, 15)
     exchange(stat_src, stat_buf, 0)
     stat_buf[me] = stat_src[...]
     exchange_wait(stat_buf, 0)
@@ -251,39 +262,47 @@
             xhat = (cv[at] - mean_c) * inv_c
             d = m * inv_c * (gain_c * dp[at] - sf_c - xhat * sg_c)
             ds[(i + 1) * 192 + 64:(i + 1) * 192 + 128, b * 128:(b + 1) * 128] = d.astype(BF)
-    for p in range(8):
-        right = jnp.concatenate(
+    part_of = lax.rem(x + y + z, 4)
+    own = part_of < 3
+    mine = part_of * 32 + lat * 2 + core
+    rows4 = [
+        jnp.concatenate(
             [ds[(4 * p + k + 1) * 192 + 64:(4 * p + k + 1) * 192 + 128, :] for k in range(4)], axis=0
         )
-        part = lax.dot_general(xs[p * 768:p * 768 + 1152, :], right, NT, preferred_element_type=F32)
-        if p == 0:
-            acc[...] = part
-        else:
-            acc[...] += part
-    here = []
-    for ky in range(3):
-        v = acc[ky * 192:(ky + 1) * 192, 0:64]
-        for k in range(1, 4):
-            v = v + acc[(ky + k) * 192:(ky + k + 1) * 192, k * 64:(k + 1) * 64]
-        here.append(v)
-    here = jnp.concatenate(here, axis=0)
-    wsrc[...] = jnp.concatenate([here[:288], here[288:]], axis=1).reshape(72, 4, 128)
-
-    def owner(la, lo):
-        half = lax.rem(la, 2)
-        return jnp.logical_or(half == 0, lo == 0), lax.div(la, 2) * 9 + half * 8 + lo
-
-    own, mine = owner(lat, lon)
-    for f in OFFSETS:
-        la, lo = peer(lat, lon, f)
-        owns, block = owner(la, lo)
-
-        @pl.when(owns)
-        def _():
-            pltpu.make_async_remote_copy(
-                src_ref=wsrc.at[block], dst_ref=wbuf.at[me], send_sem=gss.at[2], recv_sem=grs.at[2],
-                device_id=(la, lo), device_id_type=MESH,
-            ).start()
+        for p in range(8)
+    ]
+    for kx in range(3):
+        for p in range(8):
+            left = jnp.concatenate(
+                [xs[(4 * p + k) * 192 + kx * 64:(4 * p + k) * 192 + kx * 64 + 64, :] for k in range(6)], axis=0
+            )
+            part = lax.dot_general(left, rows4[p], NT, preferred_element_type=F32)
+            if p == 0:
+                acc[...] = part
+            else:
+                acc[...] += part
+        here = []
+        for ky in range(3):
+            v = acc[ky * 64:(ky + 1) * 64, 0:64]
+            for k in range(1, 4):
+                v = v + acc[(ky + k) * 64:(ky + k + 1) * 64, k * 64:(k + 1) * 64]
+            here.append(v)
+        here = jnp.concatenate(here, axis=0)
+        wsrc[kx * 32:(kx + 1) * 32] = jnp.concatenate([here[:96], here[96:]], axis=1).reshape(32, 3, 128)
+        for dx, dy in FAR_XY:
+            for dc in (1, 0):
+                la = lats[dx][dy]
+                pc = lax.rem(core + dc, 2)
+                lo = lax.rem(kx + 8 - xs_at[dx] - ys_at[dy], 4) * 2 + pc
+                block = kx * 32 + la * 2 + pc
+                send = pltpu.make_async_remote_copy(
+                    src_ref=wsrc.at[block], dst_ref=wbuf.at[me], send_sem=gss.at[2], recv_sem=grs.at[2],
+                    device_id=(la, lo), device_id_type=MESH,
+                )
+                if dx or dy or dc:
+                    send.start()
+                else:
+                    pl.when(part_of != kx)(send.start)
 
     @pl.when(own)
     def _():
@@ -293,12 +312,6 @@
     halo_d = halo_copies(ds, epd, erd, hsd, hrd)
     for c in halo_d:
         c.start()
-    for c in halo_d:
-        c.wait()
-    finish_halo(ds, erd)
-    for p in range(16):
-        r = jnp.dot(wb[...], ds[p * 384:p * 384 + 768, :], preferred_element_type=F32)
-        actt[p * 128:(p + 1) * 128, :] = r.astype(BF)
     @pl.when(own)
     def _():
         pltpu.make_async_copy(wbuf.at[pl.ds(0, 127)], wbuf.at[pl.ds(0, 127)], grs.at[2]).wait()
@@ -306,16 +319,22 @@
         for f in OFFSETS:
             pltpu.make_async_remote_copy(
                 src_ref=wgat.at[mine], dst_ref=wgat.at[mine], send_sem=gss.at[3], recv_sem=grs.at[3],
-                device_id=peer(lat, lon, f), device_id_type=MESH,
+                device_id=peer(f), device_id_type=MESH,
             ).start()
 
+    for c in halo_d:
+        c.wait()
+    finish_halo(ds, erd)
+    for p in range(16):
+        r = jnp.dot(wb[...], ds[p * 384:p * 384 + 768, :], preferred_element_type=F32)
+        actt[p * 128:(p + 1) * 128, :] = r.astype(BF)
     for b in range(2):
         sout[b] = native(actt, b)
 
     @pl.when(own)
     def _():
-        pltpu.make_async_copy(wsrc.at[pl.ds(0, 71)], wsrc.at[pl.ds(0, 71)], gss.at[2]).wait()
-        pltpu.make_async_copy(wgat.at[pl.ds(0, 71)], wgat.at[pl.ds(0, 71)], grs.at[3]).wait()
+        pltpu.make_async_copy(wsrc.at[pl.ds(0, 95)], wsrc.at[pl.ds(0, 95)], gss.at[2]).wait()
+        pltpu.make_async_copy(wgat.at[pl.ds(0, 95)], wgat.at[pl.ds(0, 95)], grs.at[3]).wait()
         pltpu.make_async_copy(wbuf.at[pl.ds(0, 127)], wbuf.at[pl.ds(0, 127)], gss.at[3]).wait()
 
     @pl.when(jnp.logical_not(own))
@@ -323,8 +342,11 @@
         pltpu.make_async_copy(wsrc, wsrc, gss.at[2]).wait()
         pltpu.make_async_copy(wgat, wgat, grs.at[3]).wait()
 
-    w = wgat[...].reshape(288, 128)
-    wgrad_out[...] = jnp.concatenate([w[:, :64], w[:, 64:]], axis=0).reshape(3, 3, 64, 64)
+    for kx in range(3):
+        w = wgat[kx * 32:(kx + 1) * 32].reshape(96, 128)
+        w = jnp.concatenate([w[:, :64], w[:, 64:]], axis=0)
+        for ky in range(3):
+            wgrad_out[ky, kx] = w[ky * 64:(ky + 1) * 64]
 
 
 def store(*refs):
@@ -355,12 +377,13 @@
             V((128, 768), BF), V((128, 768), BF),
             V((64, 128), BF), V((64, 128), BF), V((6, 64, 128), BF), V((6, 64, 128), BF),
             V((2, 128), F32), V((128, 2, 128), F32), V((1, 128), F32), V((128, 1, 128), F32),
-            V((72, 4, 128), F32), V((128, 4, 128), F32), V((1152, 256), F32), V((72, 4, 128), F32),
+            V((96, 3, 128), F32), V((128, 3, 128), F32), V((384, 256), F32), V((96, 3, 128), F32),
             V((384, 128), F32), V((32, 128), F32),
             pltpu.SemaphoreType.DMA((6,)),
             pltpu.SemaphoreType.DMA((8,)), pltpu.SemaphoreType.DMA((8,)),
             pltpu.SemaphoreType.DMA((8,)), pltpu.SemaphoreType.DMA((8,)),
             pltpu.SemaphoreType.DMA((4,)), pltpu.SemaphoreType.DMA((4,)),
+            pltpu.SemaphoreType.REGULAR,
         ],
         compiler_params=pltpu.CompilerParams(
             collective_id=0, has_side_effects=True, vmem_limit_bytes=40 * 2**20

time: 51.3 us -> 47.8 us (0.932)
  Pallas kernels: 50.3 us -> 47 us
    pallas_call x1, Pallas kernels: 48.9 us -> 45.5 us  [on_device(): pl.pallas_call(kernel, out_shape=outs, in_specs=[hbm] * 6, out_specs=[vm]...]
where the time goes in v3:
time: 47.8 us; the launch traced here: 47.6 us
  Pallas kernels  47 us (98%)
  between operations  0.64 us (1%)
    pallas_call x1, Pallas kernels, on_device(): pl.pallas_call(kernel, out_shape=outs, in_specs=[hbm] * 6, out_specs=[vm]...  45.5 us
    pallas_call x1, Pallas kernels, on_device(): pl.pallas_call(store, out_shape=outs, in_specs=[vm] * 5, out_specs=[anywh...  1.45 us

profile of v3, /device:TPU:1, one launch (start us, length us, event | category | flops | bytes accessed | tf_op | source)
XLA Modules:
  0.0 47.6 jit_solution(9353434065269523178)
XLA Ops:
  0.6 45.5 %shard_map.101 = (bf16[2,64,32,128]{3,2,1,0:T(8,128)(2,1)S(1)}, bf16[2,64,32,128]{3,2,1,0:T(8,128)(2,1)S(1)}, f32[3,3,64,64]{3,2,1,0:T(8,128)S(1)}, f32[64]{0:T(128)S(1)}, f32[64]{0:T(128)S(1)}) custom-call(bf16[2,64,32,128]{3,2,1,0:T(8,128)(2,1)} %state.1, s32[32,128]{1,0:T(8,128)} %mask_hbm.1, bf16[3,3,64,64]{3,2,1,0:T(8,128)(2,1)} %weight_hbm.1, ...), custom_call_target="tpu_custom_call" | custom-call | tf_op jit(solution)/shard_map/pallas_call | solution.py:368
  46.2 1.5 %shard_map.102 = (bf16[2,64,32,128]{3,2,1,0:T(8,128)(2,1)}, bf16[2,64,32,128]{3,2,1,0:T(8,128)(2,1)}, f32[3,3,64,64]{3,2,1,0:T(8,128)}, f32[64]{0:T(128)}, f32[64]{0:T(128)}) custom-call(bf16[2,64,32,128]{3,2,1,0:T(8,128)(2,1)S(1)} %get-tuple-element.10.refs_0_, bf16[2,64,32,128]{3,2,1,0:T(8,128)(2,1)S(1)} %get-tuple-element.11.refs_1_, ...), custom_call_target="tpu_custom_call" | custom-call | tf_op jit(solution)/shard_map/pallas_call | solution.py:392

commit v4 on v3

--- a/solution.py
+++ b/solution.py
@@ -33,7 +33,7 @@
 def kernel(
     state, mask_hbm, weight_hbm, gain_hbm, bias_hbm, cot,
     aout, sout, wgrad_out, gain_out, bias_out,
-    xin, cin, mask, weight, gain, bias, xs, ds, cv, dp, ctm, actt, wf, wb, epx, epd, erx, erd,
+    xin, cin, mask, weight, gain, bias, xs, ds, cv, dp, ctm, actt, wf, wb, wrow, wcol, rows4, epx, epd, erx, erd, cpx, cpd, crx, crd,
     stat_src, stat_buf, grad_src, grad_buf, wsrc, wbuf, acc, wgat, cols, mrow,
     dma, hsx, hrx, hsd, hrd, gss, grs, all_here,
 ):
@@ -76,6 +76,10 @@
     taps = weight[...].reshape(576, 64)
     wt = jnp.transpose(taps.astype(F32), (1, 0)).astype(BF)
     zero = jnp.zeros((64, 192), BF)
+    wrow[0:64, :] = wt[:, 0:192]
+    wrow[64:128, :] = wt[:, 384:576]
+    wcol[0:64, :] = jnp.concatenate([wt[:, 192 * k + 128:192 * k + 192] for k in range(3)], axis=1)
+    wcol[64:128, :] = jnp.concatenate([wt[:, 192 * k:192 * k + 64] for k in range(3)], axis=1)
     wf[0:64, :] = jnp.concatenate([wt, zero], axis=1)
     wf[64:128, :] = jnp.concatenate([zero, wt], axis=1)
     back = jnp.concatenate([weight[2 - t // 3, 2 - t % 3] for t in range(9)], axis=1)
@@ -92,31 +96,43 @@
 
     lane = lax.broadcasted_iota(jnp.int32, (64, 128), 1)
 
-    def shifts_and_pack(buf, epack):
+    def shifts_and_pack(buf, epack, cpack):
         packed = jnp.zeros((64, 128), BF)
+        none = jnp.zeros((64, 128), BF)
         for b in range(2):
             half = pl.ds(b * 128, 128)
             for i in range(32):
                 q = b * 32 + i
                 base = (i + 1) * 192
                 v = buf[base + 64:base + 128, half]
-                buf[base:base + 64, half] = pltpu.roll(v, 1, 1)
-                buf[base + 128:base + 192, half] = pltpu.roll(v, 127, 1)
+                buf[base:base + 64, half] = jnp.where(lane == 0, none, pltpu.roll(v, 1, 1))
+                buf[base + 128:base + 192, half] = jnp.where(lane == 127, none, pltpu.roll(v, 127, 1))
                 turned = pltpu.roll(v, (2 * q + 1) % 128, 1)
                 packed = jnp.where(lax.div(lane, 2) == q, turned, packed)
         epack[...] = packed
-
-    def halo_copies(buf, epack, erecv, ss, rs):
+        fold = jnp.zeros((16, 128), BF)
+        for g in range(4):
+            part = packed[16 * g:16 * g + 16]
+            part = pltpu.roll(part, 4 * g, 1) if g else part
+            pos = lax.rem(lane[0:16] + (128 - 4 * g), 128)
+            corner = (pos < 2) | ((pos >= 62) & (pos < 66)) | (pos >= 126)
+            fold = jnp.where(corner, part, fold)
+        cpack[...] = fold
+
+    def unfold(folded):
+        return jnp.concatenate([folded] + [pltpu.roll(folded, 128 - 4 * g, 1) for g in range(1, 4)], axis=0)
+
+    def halo_copies(buf, epack, cpack, erecv, crecv, ss, rs):
         row = lambda p: buf.at[pl.ds((p * 3 + 1) * 64, 64)]
         plan = [
+            (cpack, crecv.at[0], (south, east)),
+            (cpack, crecv.at[1], (south, west)),
+            (cpack, crecv.at[2], (north, east)),
+            (cpack, crecv.at[3], (north, west)),
             (row(1), row(33), (north, lon)),
             (row(32), row(0), (south, lon)),
             (epack, erecv.at[0], (lat, east)),
             (epack, erecv.at[1], (lat, west)),
-            (epack, erecv.at[2], (south, east)),
-            (epack, erecv.at[3], (south, west)),
-            (epack, erecv.at[4], (north, east)),
-            (epack, erecv.at[5], (north, west)),
         ]
         return [
             pltpu.make_async_remote_copy(
@@ -135,7 +151,7 @@
     def join(left, right):
         return jnp.where(lax.rem(lane, 2) == 0, pltpu.roll(right, 127, 1), pltpu.roll(left, 1, 1))
 
-    def finish_halo(buf, erecv):
+    def finish_rows(buf, crecv):
         for p, keep in ((0, lat > 0), (33, lat < 15)):
             base = p * 192
             scale = jnp.where(keep, 1.0, 0.0).astype(F32)
@@ -146,10 +162,12 @@
                 vb = v[:, b * 128:(b + 1) * 128]
                 buf[base:base + 64, half] = pltpu.roll(vb, 1, 1)
                 buf[base + 128:base + 192, half] = pltpu.roll(vb, 127, 1)
-            left, right, i = (erecv[2], erecv[3], 31) if p == 0 else (erecv[4], erecv[5], 0)
-            corner = (join(left, right).astype(F32) * scale).astype(BF)
+            left, right, i = (crecv[0], crecv[1], 31) if p == 0 else (crecv[2], crecv[3], 0)
+            corner = (join(unfold(left), unfold(right)).astype(F32) * scale).astype(BF)
             for b in range(2):
                 insert(buf, p, b, corner, b * 32 + i)
+
+    def finish_columns(buf, erecv):
         joined = join(erecv[0], erecv[1])
         for b in range(2):
             for i in range(32):
@@ -164,6 +182,8 @@
 
     def exchange_wait(buf, sem):
         pltpu.make_async_copy(buf.at[pl.ds(0, 127)], buf.at[pl.ds(0, 127)], grs.at[sem]).wait()
+
+    def exchange_sent(buf, sem):
         pltpu.make_async_copy(buf.at[pl.ds(0, 127)], buf.at[pl.ds(0, 127)], gss.at[sem]).wait()
 
     loads[0].wait()
@@ -171,10 +191,10 @@
         t = jnp.transpose(xin[b] * mask_bf[None], (1, 0, 2))
         for i in range(32):
             xs[(i + 1) * 192 + 64:(i + 1) * 192 + 128, b * 128:(b + 1) * 128] = t[i]
-    shifts_and_pack(xs, epx)
+    shifts_and_pack(xs, epx, cpx)
 
     pl.semaphore_wait(barrier, len(GREETED))
-    halo_x = halo_copies(xs, epx, erx, hsx, hrx)
+    halo_x = halo_copies(xs, epx, cpx, erx, crx, hsx, hrx)
     for c in halo_x:
         c.start()
     for a, b in GREETED:
@@ -185,30 +205,61 @@
         t = jnp.transpose(cin[b] * mask_bf[None], (1, 0, 2))
         for i in range(32):
             ctm[i * 64:(i + 1) * 64, b * 128:(b + 1) * 128] = t[i]
-    for c in halo_x:
-        c.wait()
-    finish_halo(xs, erx)
-
-    first = jnp.zeros((64, 128), F32)
+    near = jnp.zeros((64, 128), F32)
     for p in range(16):
-        r = jnp.dot(wf[...], xs[p * 384:p * 384 + 768, :], preferred_element_type=F32)
+        if p == 0:
+            r = jnp.dot(wf[:, 192:768], xs[192:768, :], preferred_element_type=F32)
+        elif p == 15:
+            r = jnp.dot(wf[:, 0:576], xs[30 * 192:33 * 192, :], preferred_element_type=F32)
+        else:
+            r = jnp.dot(wf[...], xs[p * 384:p * 384 + 768, :], preferred_element_type=F32)
         cv[p * 128:(p + 1) * 128, :] = r
         for h in range(2):
             m = mrow[2 * p + h:2 * p + h + 1, :]
-            first = first + (r[h * 64:(h + 1) * 64, :128] + r[h * 64:(h + 1) * 64, 128:]) * m
-    mean_here = jnp.sum(first, axis=1, keepdims=True) / jnp.maximum(n_local, 1.0)
-    mean_here = jnp.broadcast_to(mean_here, (64, 128))
+            near = near + (r[h * 64:(h + 1) * 64, :128] + r[h * 64:(h + 1) * 64, 128:]) * m
+    n_safe = jnp.maximum(n_local, 1.0)
+    pivot = jnp.broadcast_to(jnp.sum(near, axis=1, keepdims=True) / n_safe, (64, 128))
+    pivot_row = jnp.transpose(jnp.concatenate([pivot, jnp.zeros((64, 128), F32)], axis=0), (1, 0))[0:1]
+
+    for c in halo_x:
+        c.wait()
+    finish_rows(xs, crx)
+    top = jnp.dot(wrow[0:64, :], xs[0:192, :], preferred_element_type=F32)
+    bottom = jnp.dot(wrow[64:128, :], xs[33 * 192:34 * 192, :], preferred_element_type=F32)
+    joined = join(erx[0], erx[1])
+    place = lax.rem(lax.div(lane, 2), 32)
+    nothing = jnp.zeros((64, 128), BF)
+    above = jnp.where(place == 0, nothing, pltpu.roll(joined, 2, 1))
+    below = jnp.where(place == 31, nothing, pltpu.roll(joined, 126, 1))
+    sides = jnp.dot(wcol[...], jnp.concatenate([above, joined, below], axis=0), preferred_element_type=F32)
+    sides = jnp.where(lax.rem(lane, 2) == 0, sides[0:64], sides[64:128])
+    edge = jnp.logical_or(lane == 0, lane == 127)
+    first = jnp.zeros((64, 128), F32)
     second = jnp.zeros((64, 128), F32)
     for i in range(32):
         m = mrow[i:i + 1, :]
         for b in range(2):
-            d = cv[i * 64:(i + 1) * 64, b * 128:(b + 1) * 128] - mean_here
-            second = second + d * d * m
+            at = (pl.ds(i * 64, 64), pl.ds(b * 128, 128))
+            side = pltpu.roll(sides, (127 - 2 * (b * 32 + i)) % 128, 1)
+            v = cv[at] + jnp.where(edge, side, 0.0)
+            if i == 0:
+                v = v + top[:, b * 128:(b + 1) * 128]
+            if i == 31:
+                v = v + bottom[:, b * 128:(b + 1) * 128]
+            cv[at] = v
+            d = v - pivot
+            md = d * m
+            first = first + md
+            second = second + d * md
     row = jnp.sum(jnp.transpose(jnp.concatenate([first, second], axis=0), (1, 0)), axis=0, keepdims=True)
+    low = lax.broadcasted_iota(jnp.int32, (1, 128), 1) < 64
+    sums_here = pltpu.roll(row, 64, 1)
+    row = jnp.where(low, row + n_local * pivot_row, row - sums_here * sums_here / n_safe)
     stat_src[...] = jnp.concatenate([row, jnp.broadcast_to(n_local, (1, 128))], axis=0)
     pl.semaphore_wait(all_here, 15)
     exchange(stat_src, stat_buf, 0)
     stat_buf[me] = stat_src[...]
+    finish_columns(xs, erx)
     exchange_wait(stat_buf, 0)
     sums = stat_buf[:, 0, :]
     counts = stat_buf[:, 1, :]
@@ -218,7 +269,6 @@
     apart = sums / jnp.maximum(counts, 1.0) - mean
     between = jnp.sum(apart * apart * counts, axis=0, keepdims=True)
     var = (total + pltpu.roll(between, 64, 1)) / count
-    low = lax.broadcasted_iota(jnp.int32, (1, 128), 1) < 64
     mi = column(jnp.where(low, mean, lax.rsqrt(var + 1e-05)))
     cols[128:256, :] = mi
 
@@ -230,8 +280,7 @@
             at = (pl.ds(i * 64, 64), pl.ds(b * 128, 128))
             xhat = (cv[at] - mean_c) * inv_c
             pre = gain_c * xhat + bias_c
-            s = 1.0 / (1.0 + jnp.exp(-pre))
-            actt[at] = (pre * s).astype(BF)
+            s = 0.5 * jnp.tanh(0.5 * pre) + 0.5
             d = ctm[at].astype(F32) * (s * (1.0 + pre * (1.0 - s)))
             dp[at] = d
             bsum = bsum + d
@@ -244,6 +293,11 @@
         t = src[:, b * 128:(b + 1) * 128].reshape(32, 64, 128)
         return jnp.transpose(t, (1, 0, 2)) * mask_bf[None]
 
+    for i in range(32):
+        for b in range(2):
+            at = (pl.ds(i * 64, 64), pl.ds(b * 128, 128))
+            pre = gain_c * ((cv[at] - mean_c) * inv_c) + bias_c
+            actt[at] = (pre * (0.5 * jnp.tanh(0.5 * pre) + 0.5)).astype(BF)
     for b in range(2):
         aout[b] = native(actt, b)
 
@@ -255,28 +309,37 @@
     cols[256:384, :] = sc
     sf_c, sg_c = cols[256:320, :], cols[320:384, :]
 
+    def left_rows(p, kx):
+        return jnp.concatenate(
+            [xs[(4 * p + k) * 192 + kx * 64:(4 * p + k) * 192 + kx * 64 + 64, :] for k in range(6)], axis=0
+        )
+
     for i in range(32):
         m = mrow[i:i + 1, :]
         for b in range(2):
             at = (pl.ds(i * 64, 64), pl.ds(b * 128, 128))
             xhat = (cv[at] - mean_c) * inv_c
             d = m * inv_c * (gain_c * dp[at] - sf_c - xhat * sg_c)
-            ds[(i + 1) * 192 + 64:(i + 1) * 192 + 128, b * 128:(b + 1) * 128] = d.astype(BF)
+            d = d.astype(BF)
+            ds[(i + 1) * 192 + 64:(i + 1) * 192 + 128, b * 128:(b + 1) * 128] = d
+            rows4[i * 64:(i + 1) * 64, b * 128:(b + 1) * 128] = d
+        if i % 4 == 3:
+            p = i // 4
+            part = lax.dot_general(
+                left_rows(p, 0), rows4[p * 256:(p + 1) * 256, :], NT, preferred_element_type=F32
+            )
+            if p == 0:
+                acc[...] = part
+            else:
+                acc[...] += part
     part_of = lax.rem(x + y + z, 4)
     own = part_of < 3
     mine = part_of * 32 + lat * 2 + core
-    rows4 = [
-        jnp.concatenate(
-            [ds[(4 * p + k + 1) * 192 + 64:(4 * p + k + 1) * 192 + 128, :] for k in range(4)], axis=0
-        )
-        for p in range(8)
-    ]
     for kx in range(3):
-        for p in range(8):
-            left = jnp.concatenate(
-                [xs[(4 * p + k) * 192 + kx * 64:(4 * p + k) * 192 + kx * 64 + 64, :] for k in range(6)], axis=0
+        for p in range(8 if kx else 0):
+            part = lax.dot_general(
+                left_rows(p, kx), rows4[p * 256:(p + 1) * 256, :], NT, preferred_element_type=F32
             )
-            part = lax.dot_general(left, rows4[p], NT, preferred_element_type=F32)
             if p == 0:
                 acc[...] = part
             else:
@@ -288,7 +351,9 @@
                 v = v + acc[(ky + k) * 64:(ky + k + 1) * 64, k * 64:(k + 1) * 64]
             here.append(v)
         here = jnp.concatenate(here, axis=0)
-        wsrc[kx * 32:(kx + 1) * 32] = jnp.concatenate([here[:96], here[96:]], axis=1).reshape(32, 3, 128)
+        here = jnp.concatenate([here[:96], here[96:]], axis=1)
+        for k in range(3):
+            wsrc[kx * 32:(kx + 1) * 32, k, :] = here[32 * k:32 * k + 32]
         for dx, dy in FAR_XY:
             for dc in (1, 0):
                 la = lats[dx][dy]
@@ -308,14 +373,15 @@
     def _():
         wbuf[me] = wsrc[mine]
 
-    shifts_and_pack(ds, epd)
-    halo_d = halo_copies(ds, epd, erd, hsd, hrd)
+    shifts_and_pack(ds, epd, cpd)
+    halo_d = halo_copies(ds, epd, cpd, erd, crd, hsd, hrd)
     for c in halo_d:
         c.start()
     @pl.when(own)
     def _():
         pltpu.make_async_copy(wbuf.at[pl.ds(0, 127)], wbuf.at[pl.ds(0, 127)], grs.at[2]).wait()
-        wgat[mine] = jnp.sum(wbuf[...], axis=0)
+        quarters = [jnp.sum(wbuf[32 * k:32 * k + 32], axis=0) for k in range(4)]
+        wgat[mine] = (quarters[0] + quarters[1]) + (quarters[2] + quarters[3])
         for f in OFFSETS:
             pltpu.make_async_remote_copy(
                 src_ref=wgat.at[mine], dst_ref=wgat.at[mine], send_sem=gss.at[3], recv_sem=grs.at[3],
@@ -324,7 +390,8 @@
 
     for c in halo_d:
         c.wait()
-    finish_halo(ds, erd)
+    finish_rows(ds, crd)
+    finish_columns(ds, erd)
     for p in range(16):
         r = jnp.dot(wb[...], ds[p * 384:p * 384 + 768, :], preferred_element_type=F32)
         actt[p * 128:(p + 1) * 128, :] = r.astype(BF)
@@ -342,8 +409,10 @@
         pltpu.make_async_copy(wsrc, wsrc, gss.at[2]).wait()
         pltpu.make_async_copy(wgat, wgat, grs.at[3]).wait()
 
+    exchange_sent(stat_buf, 0)
+    exchange_sent(grad_buf, 1)
     for kx in range(3):
-        w = wgat[kx * 32:(kx + 1) * 32].reshape(96, 128)
+        w = jnp.concatenate([wgat[kx * 32:(kx + 1) * 32, k, :] for k in range(3)], axis=0)
         w = jnp.concatenate([w[:, :64], w[:, 64:]], axis=0)
         for ky in range(3):
             wgrad_out[ky, kx] = w[ky * 64:(ky + 1) * 64]
@@ -374,8 +443,9 @@
             V(big, BF), V(big, BF), V((32, 128), jnp.int32), V((3, 3, 64, 64), BF), V((64,), F32), V((64,), F32),
             V((34 * 192, 256), BF), V((34 * 192, 256), BF),
             V((2048, 256), F32), V((2048, 256), F32), V((2048, 256), BF), V((2048, 256), BF),
-            V((128, 768), BF), V((128, 768), BF),
-            V((64, 128), BF), V((64, 128), BF), V((6, 64, 128), BF), V((6, 64, 128), BF),
+            V((128, 768), BF), V((128, 768), BF), V((128, 192), BF), V((128, 192), BF), V((2048, 256), BF),
+            V((64, 128), BF), V((64, 128), BF), V((2, 64, 128), BF), V((2, 64, 128), BF),
+            V((16, 128), BF), V((16, 128), BF), V((4, 16, 128), BF), V((4, 16, 128), BF),
             V((2, 128), F32), V((128, 2, 128), F32), V((1, 128), F32), V((128, 1, 128), F32),
             V((96, 3, 128), F32), V((128, 3, 128), F32), V((384, 256), F32), V((96, 3, 128), F32),
             V((384, 128), F32), V((32, 128), F32),

time: 47.8 us -> 46.6 us (0.975)
  Pallas kernels: 47 us -> 45.7 us
    pallas_call x1, Pallas kernels: 45.5 us -> 44.2 us  [on_device(): pl.pallas_call(kernel, out_shape=outs, in_specs=[hbm] * 6, out_specs=[vm]...]
where the time goes in v4:
time: 46.6 us; the launch traced here: 46.5 us
  Pallas kernels  45.7 us (98%)
  between operations  0.8 us (2%)
    pallas_call x1, Pallas kernels, on_device(): pl.pallas_call(kernel, out_shape=outs, in_specs=[hbm] * 6, out_specs=[vm]...  44.2 us
    pallas_call x1, Pallas kernels, on_device(): pl.pallas_call(store, out_shape=outs, in_specs=[vm] * 5, out_specs=[anywh...  1.45 us

profile of v4, /device:TPU:1, one launch (start us, length us, event | category | flops | bytes accessed | tf_op | source)
XLA Modules:
  0.0 46.5 jit_solution(5305219872208320267)
XLA Ops:
  0.6 44.2 %shard_map.101 = (bf16[2,64,32,128]{3,2,1,0:T(8,128)(2,1)S(1)}, bf16[2,64,32,128]{3,2,1,0:T(8,128)(2,1)S(1)}, f32[3,3,64,64]{3,2,1,0:T(8,128)S(1)}, f32[64]{0:T(128)S(1)}, f32[64]{0:T(128)S(1)}) custom-call(bf16[2,64,32,128]{3,2,1,0:T(8,128)(2,1)} %state.1, s32[32,128]{1,0:T(8,128)} %mask_hbm.1, bf16[3,3,64,64]{3,2,1,0:T(8,128)(2,1)} %weight_hbm.1, ...), custom_call_target="tpu_custom_call" | custom-call | tf_op jit(solution)/shard_map/pallas_call | solution.py:437
  44.9 1.5 %shard_map.102 = (bf16[2,64,32,128]{3,2,1,0:T(8,128)(2,1)}, bf16[2,64,32,128]{3,2,1,0:T(8,128)(2,1)}, f32[3,3,64,64]{3,2,1,0:T(8,128)}, f32[64]{0:T(128)}, f32[64]{0:T(128)}) custom-call(bf16[2,64,32,128]{3,2,1,0:T(8,128)(2,1)S(1)} %get-tuple-element.10.refs_0_, bf16[2,64,32,128]{3,2,1,0:T(8,128)(2,1)S(1)} %get-tuple-element.11.refs_1_, ...), custom_call_target="tpu_custom_call" | custom-call | tf_op jit(solution)/shard_map/pallas_call | solution.py:462

commit v5 on v4

--- a/solution.py
+++ b/solution.py
@@ -35,7 +35,8 @@
     aout, sout, wgrad_out, gain_out, bias_out,
     xin, cin, mask, weight, gain, bias, xs, ds, cv, dp, ctm, actt, wf, wb, wrow, wcol, rows4, epx, epd, erx, erd, cpx, cpd, crx, crd,
     stat_src, stat_buf, grad_src, grad_buf, wsrc, wbuf, acc, wgat, cols, mrow,
-    dma, hsx, hrx, hsd, hrd, gss, grs, all_here,
+    count_src, count_row, count_lon, count_lat,
+    dma, hsx, hrx, hsd, hrd, gss, grs, cns, cnr, all_here,
 ):
     lat = lax.axis_index("lat")
     lon = lax.axis_index("lon")
@@ -197,6 +198,17 @@
     halo_x = halo_copies(xs, epx, cpx, erx, crx, hsx, hrx)
     for c in halo_x:
         c.start()
+    count_src[...] = jnp.broadcast_to(n_local, (1, 128))
+
+    def count_line(src, buf, at, line, sem):
+        for there in line:
+            pltpu.make_async_remote_copy(
+                src_ref=src, dst_ref=buf.at[at], send_sem=cns.at[sem], recv_sem=cnr.at[sem],
+                device_id=there, device_id_type=MESH,
+            ).start()
+        buf[at] = src[...]
+
+    count_line(count_src, count_lon, lon, [(lat, lax.rem(lon + b, 8)) for a, b in GREETED if b and not a], 0)
     for a, b in GREETED:
         if a and not b:
             pl.semaphore_signal(all_here, 1, device_id=(lax.rem(lat + a, 16), lon), device_id_type=MESH)
@@ -220,6 +232,14 @@
     n_safe = jnp.maximum(n_local, 1.0)
     pivot = jnp.broadcast_to(jnp.sum(near, axis=1, keepdims=True) / n_safe, (64, 128))
     pivot_row = jnp.transpose(jnp.concatenate([pivot, jnp.zeros((64, 128), F32)], axis=0), (1, 0))[0:1]
+
+    pltpu.make_async_copy(count_lon.at[pl.ds(0, 7)], count_lon.at[pl.ds(0, 7)], cnr.at[0]).wait()
+    sixteenth = lax.div(lax.broadcasted_iota(jnp.int32, (1, 128), 1), 16)
+    line = count_lon[0]
+    for k in range(1, 8):
+        line = jnp.where(sixteenth == k, count_lon[k], line)
+    count_row[...] = line
+    count_line(count_row, count_lat, lat, [(lax.rem(lat + a, 16), lon) for a, b in GREETED if a and not b], 1)
 
     for c in halo_x:
         c.wait()
@@ -255,18 +275,26 @@
     low = lax.broadcasted_iota(jnp.int32, (1, 128), 1) < 64
     sums_here = pltpu.roll(row, 64, 1)
     row = jnp.where(low, row + n_local * pivot_row, row - sums_here * sums_here / n_safe)
-    stat_src[...] = jnp.concatenate([row, jnp.broadcast_to(n_local, (1, 128))], axis=0)
+    stat_src[...] = row
     pl.semaphore_wait(all_here, 15)
     exchange(stat_src, stat_buf, 0)
     stat_buf[me] = stat_src[...]
+    pltpu.make_async_copy(count_lat.at[pl.ds(0, 15)], count_lat.at[pl.ds(0, 15)], cnr.at[1]).wait()
+    own_part = lax.div(lax.broadcasted_iota(jnp.int32, (8, 128), 1), 16) == lax.broadcasted_iota(jnp.int32, (8, 128), 0)
+    counts = []
+    for k in range(16):
+        one = jnp.where(own_part, jnp.broadcast_to(count_lat[k], (8, 128)), 0.0)
+        one = jnp.sum(one, axis=1, keepdims=True) * 0.0625
+        counts.append(jnp.broadcast_to(one, (8, 128)))
+    counts = jnp.concatenate(counts, axis=0)
+    count = jnp.maximum(jnp.sum(counts, axis=0, keepdims=True), 1.0)
+    weights = 1.0 / jnp.maximum(counts, 1.0)
     finish_columns(xs, erx)
     exchange_wait(stat_buf, 0)
     sums = stat_buf[:, 0, :]
-    counts = stat_buf[:, 1, :]
     total = jnp.sum(sums, axis=0, keepdims=True)
-    count = jnp.maximum(jnp.sum(counts, axis=0, keepdims=True), 1.0)
     mean = total / count
-    apart = sums / jnp.maximum(counts, 1.0) - mean
+    apart = sums * weights - mean
     between = jnp.sum(apart * apart * counts, axis=0, keepdims=True)
     var = (total + pltpu.roll(between, 64, 1)) / count
     mi = column(jnp.where(low, mean, lax.rsqrt(var + 1e-05)))
@@ -411,6 +439,8 @@
 
     exchange_sent(stat_buf, 0)
     exchange_sent(grad_buf, 1)
+    pltpu.make_async_copy(count_lon.at[pl.ds(0, 7)], count_lon.at[pl.ds(0, 7)], cns.at[0]).wait()
+    pltpu.make_async_copy(count_lat.at[pl.ds(0, 15)], count_lat.at[pl.ds(0, 15)], cns.at[1]).wait()
     for kx in range(3):
         w = jnp.concatenate([wgat[kx * 32:(kx + 1) * 32, k, :] for k in range(3)], axis=0)
         w = jnp.concatenate([w[:, :64], w[:, 64:]], axis=0)
@@ -446,13 +476,15 @@
             V((128, 768), BF), V((128, 768), BF), V((128, 192), BF), V((128, 192), BF), V((2048, 256), BF),
             V((64, 128), BF), V((64, 128), BF), V((2, 64, 128), BF), V((2, 64, 128), BF),
             V((16, 128), BF), V((16, 128), BF), V((4, 16, 128), BF), V((4, 16, 128), BF),
-            V((2, 128), F32), V((128, 2, 128), F32), V((1, 128), F32), V((128, 1, 128), F32),
+            V((1, 128), F32), V((128, 1, 128), F32), V((1, 128), F32), V((128, 1, 128), F32),
             V((96, 3, 128), F32), V((128, 3, 128), F32), V((384, 256), F32), V((96, 3, 128), F32),
             V((384, 128), F32), V((32, 128), F32),
+            V((1, 128), F32), V((1, 128), F32), V((8, 1, 128), F32), V((16, 1, 128), F32),
             pltpu.SemaphoreType.DMA((6,)),
             pltpu.SemaphoreType.DMA((8,)), pltpu.SemaphoreType.DMA((8,)),
             pltpu.SemaphoreType.DMA((8,)), pltpu.SemaphoreType.DMA((8,)),
             pltpu.SemaphoreType.DMA((4,)), pltpu.SemaphoreType.DMA((4,)),
+            pltpu.SemaphoreType.DMA((2,)), pltpu.SemaphoreType.DMA((2,)),
             pltpu.SemaphoreType.REGULAR,
         ],
         compiler_params=pltpu.CompilerParams(

time: 46.6 us -> 46.1 us (0.989)
  Pallas kernels: 45.7 us -> 45.1 us
    pallas_call x1, Pallas kernels: 44.2 us -> 43.7 us  [on_device(): pl.pallas_call(kernel, out_shape=outs, in_specs=[hbm] * 6, out_specs=[vm]...]
where the time goes in v5:
time: 46.1 us; the launch traced here: 45.9 us
  Pallas kernels  45.1 us (98%)
  between operations  0.8 us (2%)
    pallas_call x1, Pallas kernels, on_device(): pl.pallas_call(kernel, out_shape=outs, in_specs=[hbm] * 6, out_specs=[vm]...  43.7 us
    pallas_call x1, Pallas kernels, on_device(): pl.pallas_call(store, out_shape=outs, in_specs=[vm] * 5, out_specs=[anywh...  1.45 us

profile of v5, /device:TPU:1, one launch (start us, length us, event | category | flops | bytes accessed | tf_op | source)
XLA Modules:
  0.0 45.9 jit_solution(16529149093716223491)
XLA Ops:
  0.6 43.7 %shard_map.101 = (bf16[2,64,32,128]{3,2,1,0:T(8,128)(2,1)S(1)}, bf16[2,64,32,128]{3,2,1,0:T(8,128)(2,1)S(1)}, f32[3,3,64,64]{3,2,1,0:T(8,128)S(1)}, f32[64]{0:T(128)S(1)}, f32[64]{0:T(128)S(1)}) custom-call(bf16[2,64,32,128]{3,2,1,0:T(8,128)(2,1)} %state.1, s32[32,128]{1,0:T(8,128)} %mask_hbm.1, bf16[3,3,64,64]{3,2,1,0:T(8,128)(2,1)} %weight_hbm.1, ...), custom_call_target="tpu_custom_call" | custom-call | tf_op jit(solution)/shard_map/pallas_call | solution.py:467
  44.3 1.5 %shard_map.102 = (bf16[2,64,32,128]{3,2,1,0:T(8,128)(2,1)}, bf16[2,64,32,128]{3,2,1,0:T(8,128)(2,1)}, f32[3,3,64,64]{3,2,1,0:T(8,128)}, f32[64]{0:T(128)}, f32[64]{0:T(128)}) custom-call(bf16[2,64,32,128]{3,2,1,0:T(8,128)(2,1)S(1)} %get-tuple-element.10.refs_0_, bf16[2,64,32,128]{3,2,1,0:T(8,128)(2,1)S(1)} %get-tuple-element.11.refs_1_, ...), custom_call_target="tpu_custom_call" | custom-call | tf_op jit(solution)/shard_map/pallas_call | solution.py:494

commit v6 on v5

--- a/solution.py
+++ b/solution.py
@@ -34,7 +34,7 @@
     state, mask_hbm, weight_hbm, gain_hbm, bias_hbm, cot,
     aout, sout, wgrad_out, gain_out, bias_out,
     xin, cin, mask, weight, gain, bias, xs, ds, cv, dp, ctm, actt, wf, wb, wrow, wcol, rows4, epx, epd, erx, erd, cpx, cpd, crx, crd,
-    stat_src, stat_buf, grad_src, grad_buf, wsrc, wbuf, acc, wgat, cols, mrow,
+    stat_src, stat_buf, grad_src, grad_buf, wsrc, wbuf, accs, wgat, cols, mrow,
     count_src, count_row, count_lon, count_lat,
     dma, hsx, hrx, hsd, hrd, gss, grs, cns, cnr, all_here,
 ):
@@ -353,18 +353,20 @@
             rows4[i * 64:(i + 1) * 64, b * 128:(b + 1) * 128] = d
         if i % 4 == 3:
             p = i // 4
-            part = lax.dot_general(
-                left_rows(p, 0), rows4[p * 256:(p + 1) * 256, :], NT, preferred_element_type=F32
-            )
-            if p == 0:
-                acc[...] = part
-            else:
-                acc[...] += part
+            for kx in range(2):
+                part = lax.dot_general(
+                    left_rows(p, kx), rows4[p * 256:(p + 1) * 256, :], NT, preferred_element_type=F32
+                )
+                if p == 0:
+                    accs[kx] = part
+                else:
+                    accs[kx] += part
     part_of = lax.rem(x + y + z, 4)
     own = part_of < 3
     mine = part_of * 32 + lat * 2 + core
     for kx in range(3):
-        for p in range(8 if kx else 0):
+        acc = accs.at[kx]
+        for p in range(8 if kx == 2 else 0):
             part = lax.dot_general(
                 left_rows(p, kx), rows4[p * 256:(p + 1) * 256, :], NT, preferred_element_type=F32
             )
@@ -477,7 +479,7 @@
             V((64, 128), BF), V((64, 128), BF), V((2, 64, 128), BF), V((2, 64, 128), BF),
             V((16, 128), BF), V((16, 128), BF), V((4, 16, 128), BF), V((4, 16, 128), BF),
             V((1, 128), F32), V((128, 1, 128), F32), V((1, 128), F32), V((128, 1, 128), F32),
-            V((96, 3, 128), F32), V((128, 3, 128), F32), V((384, 256), F32), V((96, 3, 128), F32),
+            V((96, 3, 128), F32), V((128, 3, 128), F32), V((3, 384, 256), F32), V((96, 3, 128), F32),
             V((384, 128), F32), V((32, 128), F32),
             V((1, 128), F32), V((1, 128), F32), V((8, 1, 128), F32), V((16, 1, 128), F32),
             pltpu.SemaphoreType.DMA((6,)),

time: 46.1 us -> 45 us (0.976)
  Pallas kernels: 45.1 us -> 44.2 us
    pallas_call x1, Pallas kernels: 43.7 us -> 42.7 us  [on_device(): pl.pallas_call(kernel, out_shape=outs, in_specs=[hbm] * 6, out_specs=[vm]...]
where the time goes in v6:
time: 45 us; the launch traced here: 44.8 us
  Pallas kernels  44.2 us (98%)
  between operations  0.64 us (1%)
    pallas_call x1, Pallas kernels, on_device(): pl.pallas_call(kernel, out_shape=outs, in_specs=[hbm] * 6, out_specs=[vm]...  42.7 us
    pallas_call x1, Pallas kernels, on_device(): pl.pallas_call(store, out_shape=outs, in_specs=[vm] * 5, out_specs=[anywh...  1.45 us

profile of v6, /device:TPU:1, one launch (start us, length us, event | category | flops | bytes accessed | tf_op | source)
XLA Modules:
  0.0 44.8 jit_solution(10071867066341806877)
XLA Ops:
  0.6 42.7 %shard_map.101 = (bf16[2,64,32,128]{3,2,1,0:T(8,128)(2,1)S(1)}, bf16[2,64,32,128]{3,2,1,0:T(8,128)(2,1)S(1)}, f32[3,3,64,64]{3,2,1,0:T(8,128)S(1)}, f32[64]{0:T(128)S(1)}, f32[64]{0:T(128)S(1)}) custom-call(bf16[2,64,32,128]{3,2,1,0:T(8,128)(2,1)} %state.1, s32[32,128]{1,0:T(8,128)} %mask_hbm.1, bf16[3,3,64,64]{3,2,1,0:T(8,128)(2,1)} %weight_hbm.1, ...), custom_call_target="tpu_custom_call" | custom-call | tf_op jit(solution)/shard_map/pallas_call | solution.py:469
  43.4 1.5 %shard_map.102 = (bf16[2,64,32,128]{3,2,1,0:T(8,128)(2,1)}, bf16[2,64,32,128]{3,2,1,0:T(8,128)(2,1)}, f32[3,3,64,64]{3,2,1,0:T(8,128)}, f32[64]{0:T(128)}, f32[64]{0:T(128)}) custom-call(bf16[2,64,32,128]{3,2,1,0:T(8,128)(2,1)S(1)} %get-tuple-element.10.refs_0_, bf16[2,64,32,128]{3,2,1,0:T(8,128)(2,1)S(1)} %get-tuple-element.11.refs_1_, ...), custom_call_target="tpu_custom_call" | custom-call | tf_op jit(solution)/shard_map/pallas_call | solution.py:496
